TPU v7x, 32 devices: a whole 2x2x4 slice. The times are simulated.
32 devices in a mesh: wide: 8 (over z, x), narrow: 4 (over y, core).
Axes of the slice: x: 2, y: 2, z: 4, core: 2. Of those that a mesh axis runs over, the one named last changes fastest.
Arguments:
- tokens: bfloat16 [25216, 768], P(('wide', 'narrow')), may hold values from -6 to 6
- patch_mask: int32 [25216], P(('wide', 'narrow')), may hold values from 0 to 1, as said below
- cotangent: bfloat16 [25216, 768], P(('wide', 'narrow')), may hold values from -6 to 6
- mask_token: bfloat16 [768], replicated, may hold values from -6 to 6
- first_gain: bfloat16 [768], replicated, may hold values from 0.5 to 1.5
- first_bias: bfloat16 [768], replicated, may hold values from -2 to 2
- qkv_weight: bfloat16 [768, 3, 768], P(None, None, 'narrow'), may hold values from -0.3125 to 0.3125
- query_bias: bfloat16 [768], P('narrow'), may hold values from -2 to 2
- value_bias: bfloat16 [768], P('narrow'), may hold values from -2 to 2
- position_bias: bfloat16 [12, 197, 197], P('narrow'), may hold values from -3 to 3
- output_weight: bfloat16 [768, 768], P('narrow'), may hold values from -0.875 to 0.875
- output_bias: bfloat16 [768], replicated, may hold values from -2 to 2
- attention_scale: bfloat16 [768], replicated, may hold values from 0.5 to 1.5
- second_gain: bfloat16 [768], replicated, may hold values from 0.5 to 1.5
- second_bias: bfloat16 [768], replicated, may hold values from -2 to 2
- up_weight: bfloat16 [768, 3072], P(None, 'narrow'), may hold values from -0.21875 to 0.21875
- up_bias: bfloat16 [3072], P('narrow'), may hold values from -2 to 2
- down_weight: bfloat16 [3072, 768], P('narrow'), may hold values from -0.109375 to 0.109375
- down_bias: bfloat16 [768], replicated, may hold values from -2 to 2
- feedforward_scale: bfloat16 [768], replicated, may hold values from 0.5 to 1.5
Outputs:
- layer_out: bfloat16 [25216, 768], P(('wide', 'narrow'))
- input_grad: float32 [25216, 768], P(('wide', 'narrow'))
- mask_token_grad: float32 [768], replicated
- first_gain_grad: float32 [768], replicated
- first_bias_grad: float32 [768], replicated
- qkv_weight_grad: float32 [768, 3, 768], P(None, None, 'narrow')
- query_bias_grad: float32 [768], P('narrow')
- value_bias_grad: float32 [768], P('narrow')
- position_bias_grad: float32 [12, 197, 197], P('narrow')
- output_weight_grad: float32 [768, 768], P('narrow')
- output_bias_grad: float32 [768], replicated
- attention_scale_grad: float32 [768], replicated
- second_gain_grad: float32 [768], replicated
- second_bias_grad: float32 [768], replicated
- up_weight_grad: float32 [768, 3072], P(None, 'narrow')
- up_bias_grad: float32 [3072], P('narrow')
- down_weight_grad: float32 [3072, 768], P('narrow')
- down_bias_grad: float32 [768], replicated
- feedforward_scale_grad: float32 [768], replicated
Inputs may be any that keep to these rules, and one draw needn't show every extreme that they name: `patch_mask`: the first row of each image (its class token) is 0; each image has 79 to 156 of its other 196 rows at 1.
All inputs are finite; a program needn't handle non-finite values.
Results may differ from a plain program's by a relative error of at most 0.019.
The roundings to bfloat16 on the way count: a program that leaves them out, or rounds other values in their place, can miss the bound.
Values may be sent and summed in bfloat16 or wider, within the bound.
No kernel may reach another device: no remote copies, remote signals or barrier semaphores. Data moves between devices by JAX's collectives and lax.ppermute only.
A program may use at most 192 MiB of HBM per device.

v0:
```python
import jax
import jax.numpy as jnp
from jax import lax
from jax.sharding import PartitionSpec as P

HEAD_DIM = 64
LEN = 197


EPSILON = 1e-06
HALF_ROOT = 0.7071067811865476
DENSITY_FACTOR = 0.3989422804014327


def norm_parts(values):
    average = jnp.mean(values, -1, keepdims=True)
    centered = values - average
    inverse_dev = lax.rsqrt(jnp.mean(centered * centered, -1, keepdims=True) + EPSILON)
    return (centered * inverse_dev, inverse_dev)


def norm_back(grad_rows, normed, inverse_dev, gain):
    scaled = grad_rows * gain
    return inverse_dev * (
        scaled
        - jnp.mean(scaled, -1, keepdims=True)
        - normed * jnp.mean(scaled * normed, -1, keepdims=True)
    )


def gelu_slope(values):
    normal_cdf = 0.5 * (1.0 + lax.erf(values * HALF_ROOT))
    normal_pdf = jnp.exp(-0.5 * values * values) * DENSITY_FACTOR
    return normal_cdf + values * normal_pdf


def per_device(
    tokens,
    patch_mask,
    cotangent,
    mask_token,
    first_gain,
    first_bias,
    qkv_weight,
    query_bias,
    value_bias,
    position_bias,
    output_weight,
    output_bias,
    attention_scale,
    second_gain,
    second_bias,
    up_weight,
    up_bias,
    down_weight,
    down_bias,
    feedforward_scale,
):
    shard_rows, model_width = tokens.shape
    local_width = qkv_weight.shape[2]
    head_count = local_width // HEAD_DIM
    score_scale = HEAD_DIM ** (-0.5)
    bias_table = position_bias.astype(jnp.float32)[None]
    masked = (patch_mask == 1)[:, None]
    started = jnp.where(masked, mask_token.astype(jnp.float32)[None, :], tokens.astype(jnp.float32))
    normed_one, inverse_one = norm_parts(started)
    gain_one = first_gain.astype(jnp.float32)
    first_norm = (normed_one * gain_one + first_bias.astype(jnp.float32)).astype(jnp.bfloat16)
    qkv_flat = qkv_weight.reshape(model_width, 3 * local_width)
    qkv_shift = jnp.concatenate(
        [
            query_bias.astype(jnp.float32),
            jnp.zeros((local_width,), jnp.float32),
            value_bias.astype(jnp.float32),
        ]
    )
    first_all = lax.all_gather(first_norm, "narrow", axis=0, tiled=True)
    triple = (jnp.dot(first_all, qkv_flat, preferred_element_type=jnp.float32) + qkv_shift).astype(
        jnp.bfloat16
    )
    group_rows = triple.shape[0]
    image_count = group_rows // LEN
    split = triple.reshape(image_count, LEN, 3, head_count, HEAD_DIM)
    queries = split[:, :, 0]
    key_rows = split[:, :, 1]
    value_rows = split[:, :, 2]
    scores = (
        jnp.einsum("iqhd,ikhd->ihqk", queries, key_rows, preferred_element_type=jnp.float32)
        * score_scale
    )
    scores = scores + bias_table
    log_total = jax.nn.logsumexp(scores, axis=-1, keepdims=True)
    probabilities = jnp.exp(scores - log_total)
    context = jnp.einsum(
        "ihqk,ikhd->iqhd",
        probabilities.astype(jnp.bfloat16),
        value_rows,
        preferred_element_type=jnp.float32,
    )
    context = context.reshape(group_rows, local_width).astype(jnp.bfloat16)
    attention_terms = lax.psum_scatter(
        jnp.dot(context, output_weight, preferred_element_type=jnp.float32).astype(jnp.bfloat16),
        "narrow",
        scatter_dimension=0,
        tiled=True,
    ).astype(jnp.float32)
    attention_branch = attention_terms + output_bias.astype(jnp.float32)
    scale_one = attention_scale.astype(jnp.float32)
    middle = started + scale_one * attention_branch
    normed_two, inverse_two = norm_parts(middle)
    gain_two = second_gain.astype(jnp.float32)
    second_norm = (normed_two * gain_two + second_bias.astype(jnp.float32)).astype(jnp.bfloat16)
    second_all = lax.all_gather(second_norm, "narrow", axis=0, tiled=True)
    preact = jnp.dot(second_all, up_weight, preferred_element_type=jnp.float32) + up_bias.astype(
        jnp.float32
    )
    activated = jax.nn.gelu(preact, approximate=False).astype(jnp.bfloat16)
    feed_terms = lax.psum_scatter(
        jnp.dot(activated, down_weight, preferred_element_type=jnp.float32).astype(jnp.bfloat16),
        "narrow",
        scatter_dimension=0,
        tiled=True,
    ).astype(jnp.float32)
    feed_branch = feed_terms + down_bias.astype(jnp.float32)
    scale_two = feedforward_scale.astype(jnp.float32)
    layer_out = (middle + scale_two * feed_branch).astype(jnp.bfloat16)
    grad_rows = cotangent.astype(jnp.float32)
    feed_grad = (scale_two * grad_rows).astype(jnp.bfloat16)
    scale_two_grad = jnp.sum(grad_rows * feed_branch, 0)
    down_bias_grad = jnp.sum(feed_grad.astype(jnp.float32), 0)
    feed_grad_all = lax.all_gather(feed_grad, "narrow", axis=0, tiled=True)
    down_weight_grad = jnp.einsum(
        "gf,gd->fd", activated, feed_grad_all, preferred_element_type=jnp.float32
    )
    activated_grad = jnp.einsum(
        "gd,fd->gf", feed_grad_all, down_weight, preferred_element_type=jnp.float32
    )
    preact_grad = (activated_grad * gelu_slope(preact)).astype(jnp.bfloat16)
    up_bias_grad = jnp.sum(preact_grad.astype(jnp.float32), 0)
    up_weight_grad = jnp.einsum(
        "gd,gf->df", second_all, preact_grad, preferred_element_type=jnp.float32
    )
    second_grad = lax.psum_scatter(
        jnp.einsum("gf,df->gd", preact_grad, up_weight, preferred_element_type=jnp.float32).astype(
            jnp.bfloat16
        ),
        "narrow",
        scatter_dimension=0,
        tiled=True,
    ).astype(jnp.float32)
    second_gain_grad = jnp.sum(second_grad * normed_two, 0)
    second_bias_grad = jnp.sum(second_grad, 0)
    middle_grad = grad_rows + norm_back(second_grad, normed_two, inverse_two, gain_two)
    scale_one_grad = jnp.sum(middle_grad * attention_branch, 0)
    attention_grad = (scale_one * middle_grad).astype(jnp.bfloat16)
    output_bias_grad = jnp.sum(attention_grad.astype(jnp.float32), 0)
    attention_grad_all = lax.all_gather(attention_grad, "narrow", axis=0, tiled=True)
    output_weight_grad = jnp.einsum(
        "ge,gd->ed", context, attention_grad_all, preferred_element_type=jnp.float32
    )
    context_grad = jnp.einsum(
        "gd,ed->ge", attention_grad_all, output_weight, preferred_element_type=jnp.float32
    )
    context_grad = context_grad.astype(jnp.bfloat16).reshape(image_count, LEN, head_count, HEAD_DIM)
    scores_again = (
        jnp.einsum("iqhd,ikhd->ihqk", queries, key_rows, preferred_element_type=jnp.float32)
        * score_scale
    )
    weights_again = jnp.exp(scores_again + bias_table - log_total)
    values_grad = jnp.einsum(
        "ihqk,iqhd->ikhd",
        weights_again.astype(jnp.bfloat16),
        context_grad,
        preferred_element_type=jnp.float32,
    )
    probability_grad = jnp.einsum(
        "iqhd,ikhd->ihqk", context_grad, value_rows, preferred_element_type=jnp.float32
    )
    score_grad = weights_again * (
        probability_grad - jnp.sum(probability_grad * weights_again, -1, keepdims=True)
    )
    score_grad = score_grad.astype(jnp.bfloat16)
    position_bias_grad = jnp.sum(score_grad.astype(jnp.float32), 0)
    queries_grad = (
        jnp.einsum("ihqk,ikhd->iqhd", score_grad, key_rows, preferred_element_type=jnp.float32)
        * score_scale
    )
    keys_grad = (
        jnp.einsum("ihqk,iqhd->ikhd", score_grad, queries, preferred_element_type=jnp.float32)
        * score_scale
    )
    triple_grad = jnp.stack([queries_grad, keys_grad, values_grad], 2).reshape(
        group_rows, 3, local_width
    )
    triple_grad = triple_grad.astype(jnp.bfloat16)
    query_bias_grad = jnp.sum(triple_grad[:, 0].astype(jnp.float32), 0)
    value_bias_grad = jnp.sum(triple_grad[:, 2].astype(jnp.float32), 0)
    qkv_weight_grad = jnp.einsum(
        "gd,gtc->dtc", first_all, triple_grad, preferred_element_type=jnp.float32
    )
    first_grad = lax.psum_scatter(
        jnp.einsum(
            "gtc,dtc->gd", triple_grad, qkv_weight, preferred_element_type=jnp.float32
        ).astype(jnp.bfloat16),
        "narrow",
        scatter_dimension=0,
        tiled=True,
    ).astype(jnp.float32)
    first_gain_grad = jnp.sum(first_grad * normed_one, 0)
    first_bias_grad = jnp.sum(first_grad, 0)
    started_grad = middle_grad + norm_back(first_grad, normed_one, inverse_one, gain_one)
    input_grad = jnp.where(masked, 0.0, started_grad)
    token_grad = jnp.sum(jnp.where(masked, started_grad, 0.0), 0)
    row_sums = lax.psum(
        (
            token_grad,
            first_gain_grad,
            first_bias_grad,
            output_bias_grad,
            scale_one_grad,
            second_gain_grad,
            second_bias_grad,
            down_bias_grad,
            scale_two_grad,
        ),
        "narrow",
    )
    summed = lax.psum(
        (
            row_sums[0],
            row_sums[1],
            row_sums[2],
            qkv_weight_grad,
            query_bias_grad,
            value_bias_grad,
            position_bias_grad,
            output_weight_grad,
            row_sums[3],
            row_sums[4],
            row_sums[5],
            row_sums[6],
            up_weight_grad,
            up_bias_grad,
            down_weight_grad,
            row_sums[7],
            row_sums[8],
        ),
        "wide",
    )
    return (
        layer_out,
        input_grad,
        summed[0],
        summed[1],
        summed[2],
        summed[3],
        summed[4],
        summed[5],
        summed[6],
        summed[7],
        summed[8],
        summed[9],
        summed[10],
        summed[11],
        summed[12],
        summed[13],
        summed[14],
        summed[15],
        summed[16],
    )


def solution(mesh):
    in_specs = (
        P(("wide", "narrow"), None),
        P(("wide", "narrow")),
        P(("wide", "narrow"), None),
        P(),
        P(),
        P(),
        P(None, None, "narrow"),
        P("narrow"),
        P("narrow"),
        P("narrow", None, None),
        P("narrow", None),
        P(),
        P(),
        P(),
        P(),
        P(None, "narrow"),
        P("narrow"),
        P("narrow", None),
        P(),
        P(),
    )
    out_specs = (
        P(("wide", "narrow"), None),
        P(("wide", "narrow"), None),
        P(),
        P(),
        P(),
        P(None, None, "narrow"),
        P("narrow"),
        P("narrow"),
        P("narrow", None, None),
        P("narrow", None),
        P(),
        P(),
        P(),
        P(),
        P(None, "narrow"),
        P("narrow"),
        P("narrow", None),
        P(),
        P(),
    )
    return jax.shard_map(
        per_device, mesh=mesh, in_specs=in_specs, out_specs=out_specs, check_vma=False
    )
```

profile of v0, /device:TPU:0, one launch (start us, length us, event | category | flops | bytes accessed | tf_op | source)
XLA Modules:
  0.0 720.3 jit_solution(4208180064320233361)
XLA Ops:
  19.5 37.6 %all-gather.9.cloned.1.call-done = bf16[4,788,768]{2,1,0:T(8,128)(2,1)} async-done(((bf16[1,788,768]{2,1,0:T(8,128)(2,1)}), bf16[4,788,768]{2,1,0:T(8,128)(2,1)}) %all-gather.9.cloned.1.call-update) | async-done | bytes 4841488 | tf_op jit(solution)/shard_map/all_gather | solution.py:77
  57.0 4.6 reshape.135
  61.6 7.8 %add_convert_fusion = bf16[3152,576]{0,1:T(8,128)(2,1)} fusion(bf16[3152,768]{1,0:T(8,128)(2,1)} %reshape.135, bf16[768,576]{0,1:T(8,128)(2,1)} %bitcast.103, f32[576]{0:T(1024)S(1)} %pad_maximum_fusion), kind=kOutput, calls=%fused_computation.35 | convolution fusion | flops 2792318976 | bytes 9359616 | tf_op jit(solution)/shard_map/dot_general | solution.py:78
  69.4 15.6 %reshape.132 = bf16[16,197,3,3,64]{1,0,4,3,2:T(8,128)(2,1)} reshape(bf16[3152,576]{0,1:T(8,128)(2,1)} %add_convert_fusion) | data formatting | bytes 7262208 | tf_op jit(solution)/shard_map/reshape | solution.py:83
  105.0 5.0 convolution_convert_fusion.2
  110.1 46.5 %fusion = bf16[792,768]{1,0:T(8,128)(2,1)} fusion(bf16[3152,768]{1,0:T(8,128)(2,1)} %convolution_convert_fusion.2), kind=kCustom, calls=%all-reduce-scatter | all-reduce-scatter fusion | flops 2433025 | bytes 6058496
  160.0 7.2 concatenate.6
  173.3 4.8 reshape.139
  178.1 37.2 %all-gather.11.cloned.1.call-done = bf16[4,788,768]{2,1,0:T(8,128)(2,1)} async-done(((bf16[1,788,768]{2,1,0:T(8,128)(2,1)}), bf16[4,788,768]{2,1,0:T(8,128)(2,1)}) %all-gather.11.cloned.1.call-update) | async-done | bytes 4841488 | tf_op jit(solution)/shard_map/all_gather | solution.py:113
  219.8 26.3 %fusion.6 = (bf16[3152,768]{1,0:T(8,128)(2,1)}, f32[3152,768]{1,0:T(8,128)S(1)}) fusion(f32[768]{0:T(1024)S(1)} %convert_element_type.154, bf16[3152,768]{1,0:T(8,128)(2,1)} %reshape.137, bf16[768,768]{1,0:T(8,128)(2,1)S(1)} %copy-done), kind=kOutput, calls=%fused_computation.10 | convolution fusion | flops 3878019072 | bytes 20548608 | tf_op jit(solution)/shard_map/dot_general | solution.py:114
  246.1 7.4 %convert_reduce_fusion.1 = (f32[768]{0:T(1024)S(1)}, bf16[3152,768]{1,0:T(8,128)(2,1)S(1)}) fusion(f32[3152,768]{1,0:T(8,128)S(1)} %get-tuple-element.94, f32[768]{0:T(1024)S(1)} %convert_element_type.154, bf16[3152,768]{1,0:T(8,128)(2,1)S(1)} %bitcast.98, bf16[768,768]{1,0:T(8,128)(2,1)S(1)} %copy-done.47), kind=kOutput, calls=%fused_computation.18 | convolution fusion | flops 3749719296 | bytes 20551680 | tf_op jit(solution)/shard_map/gd,fd->gf/dot_general | solution.py:135
  255.7 5.8 convolution_convert_fusion
  261.5 46.3 %fusion.2 = bf16[792,768]{1,0:T(8,128)(2,1)} fusion(bf16[3152,768]{1,0:T(8,128)(2,1)} %convolution_convert_fusion), kind=kCustom, calls=%all-reduce-scatter.2 | all-reduce-scatter fusion | flops 2433025 | bytes 6058496
  310.7 7.1 concatenate.8
  327.7 9.1 %convolution_convert_fusion.1 = bf16[3152,768]{1,0:T(8,128)(2,1)} fusion(bf16[3152,768]{1,0:T(8,128)(2,1)} %get-tuple-element.93, bf16[768,768]{1,0:T(8,128)(2,1)} %param.37), kind=kOutput, calls=%fused_computation.37 | convolution fusion | flops 3720671232 | bytes 10862592 | tf_op jit(solution)/shard_map/dot_general | solution.py:119
  336.8 8.6 %fusion.62 = f32[768,768]{1,0:T(8,128)} fusion(bf16[3152,768]{1,0:T(8,128)(2,1)} %get-tuple-element.93, bf16[3152,768]{1,0:T(8,128)(2,1)S(1)} %bitcast.100), kind=kOutput, calls=%fused_computation.126 | convolution fusion | flops 3718250496 | bytes 12042240 | tf_op jit(solution)/shard_map/gf,gd->fd/dot_general | solution.py:132
  345.3 9.5 %fusion.61 = f32[768,768]{1,0:T(8,128)} fusion(bf16[3152,768]{1,0:T(8,128)(2,1)} %reshape.137, bf16[3152,768]{1,0:T(8,128)(2,1)} %copy-done.50), kind=kOutput, calls=%fused_computation.125 | convolution fusion | flops 3718250496 | bytes 12042240 | tf_op jit(solution)/shard_map/gd,gf->df/dot_general | solution.py:140
  354.9 15.1 %all-gather.15.cloned.1.call-done = bf16[4,788,768]{2,1,0:T(8,128)(2,1)} async-done(((bf16[1,788,768]{2,1,0:T(8,128)(2,1)}), bf16[4,788,768]{2,1,0:T(8,128)(2,1)}) %all-gather.15.cloned.1.call-update) | async-done | bytes 4841488 | tf_op jit(solution)/shard_map/all_gather | solution.py:157
  370.0 4.6 reshape.141
  374.6 4.9 fusion.60
  382.3 6.7 reshape.133
  389.1 8.2 %fusion.43 = bf16[16,197,3,64]{1,3,2,0:T(8,128)(2,1)} fusion(bf16[16,197,3,64]{1,0,3,2:T(8,128)(2,1)} %reshape.133, f32[16,3,197,197]{2,3,1,0:T(8,128)} %copy-done.2, f32[16,3,197]{2,1,0:T(4,128)S(1)} %copy-done.25, f32[3,197,197]{1,2,0:T(8,128)S(1)} %copy-done.7), kind=kOutput, calls=%fused_computation.95 | convolution fusion | flops 246499008 | bytes 10375596 | tf_op jit(solution)/shard_map/ihqk,iqhd->ikhd/dot_general | solution.py:170
  397.3 8.5 %multiply_reduce_fusion = (f32[16,3,197]{2,1,0:T(4,128)S(1)}, f32[16,3,197,197]{2,3,1,0:T(8,128)S(1)}) fusion(f32[16,3,197,197]{2,3,1,0:T(8,128)} %copy-done.2, f32[16,3,197]{2,1,0:T(4,128)S(1)} %copy-done.25, f32[3,197,197]{1,2,0:T(8,128)S(1)} %copy-done.7, bf16[16,197,1,3,64]{1,0,4,3,2:T(8,128)(2,1)S(1)} %copy-done.13, bf16[16,197,3,64]{1,0,3,2:T(8,128)(2,1)} %reshape.133), kind=kOutput, calls=%fused_computation.4 | convolution fusion | flops 247747200 | bytes 17864748 | tf_op jit(solution)/shard_map/iqhd,ikhd->ihqk/dot_general | solution.py:176
  439.8 8.1 %fusion.63 = f32[768,576]{0,1} fusion(bf16[3152,576]{0,1:T(8,128)(2,1)S(1)} %bitcast.102, bf16[3152,768]{1,0:T(8,128)(2,1)} %reshape.135), kind=kOutput, calls=%fused_computation.127 | convolution fusion | flops 2788687872 | bytes 10242048
  447.9 8.4 %bitcast_convert_fusion = bf16[3152,768]{1,0:T(8,128)(2,1)} fusion(bf16[3152,3,192]{0,2,1:T(8,128)(2,1)} %copy-done.27, bf16[768,3,192]{0,2,1:T(8,128)(2,1)} %param.26), kind=kOutput, calls=%fused_computation.17 | convolution fusion | flops 2791108608 | bytes 9357312 | tf_op jit(solution)/shard_map/gtc,dtc->gd/dot_general | solution.py:202
  456.3 86.4 %fusion.57 = (bf16[792,768]{1,0:T(8,128)(2,1)}, bf16[792,768]{1,0:T(8,128)(2,1)}) fusion(bf16[3152,768]{1,0:T(8,128)(2,1)} %convolution_convert_fusion.1, bf16[3152,768]{1,0:T(8,128)(2,1)} %bitcast_convert_fusion), kind=kCustom, calls=%all-reduce-scatter.4 | all-reduce-scatter fusion | flops 4866049 | bytes 12116480
  551.9 7.2 concatenate.9
  559.1 7.2 %concatenate.7 = bf16[804,768]{1,0:T(8,128)(2,1)} concatenate(bf16[12,768]{1,0:T(8,128)(2,1)S(1)} %collective-permute-done.1, bf16[792,768]{1,0:T(8,128)(2,1)} %get-tuple-element.78), dimensions={0} | concatenate | bytes 2469888
  569.4 6.6 fusion.36
  576.0 10.9 %all-reduce.10 = (f32[768]{0:T(1024)S(1)}, f32[768]{0:T(1024)S(1)}, f32[768]{0:T(1024)S(1)}, f32[768]{0:T(1024)S(1)}, f32[768]{0:T(1024)S(1)}, /*index=5*/f32[76...) all-reduce(f32[768]{0:T(1024)S(1)} %get-tuple-element.89, ...), channel_id=1, replica_groups=mesh['wide'=8,'narrow'=4] {'narrow'}, use_global_device_ids=true, to_apply=%region_16.17 | all-reduce | flops 6912 | bytes 55296 | tf_op jit(solution)/shard_map/psum | solution.py:214
  586.9 39.3 %all-reduce.8 = (f32[768]{0:T(1024)}, f32[768]{0:T(1024)}, f32[768]{0:T(1024)}, f32[192]{0:T(256)}, f32[192]{0:T(256)}, /*index=5*/f32[768]{0:T(1024)}, f32[768]...) all-reduce(f32[768]{0:T(1024)S(1)} %get-tuple-element.67, ...), channel_id=1, replica_groups=mesh['wide'=8,'narrow'=4] {'wide'}, use_global_device_ids=true, to_apply=%region_17.18 | all-reduce | flops 8064 | bytes 64512 | tf_op jit(solution)/shard_map/psum | solution.py:228
  629.6 74.2 %all-reduce.14.cloned.1.call-done = (f32[768,3,192]{0,2,1:T(8,128)}, f32[3,197,197]{1,2,0:T(8,128)}, f32[192,768]{1,0:T(8,128)}, f32[768,768]{1,0:T(8,128)}, f32[768,768]{1,0:T(8,128)}) async-done(((f32[768,3,192]{0,2,1:T(8,128)}, f32[3,197,197]{1,2,0:T(8,128)}, f32[192,768]{1,0:T(8,128)}, f32[768,768]{1,0:T(8,128)}, f32[768,768]{1,0:T(8,128)}), (f32[768,3,192]{0,2,1:T(8,128)}, f32[3,197,197]{1,2,0:T(8,128)}, ...) | async-done | bytes 7543612 | tf_op jit(solution)/shard_map/psum | solution.py:228
  (207 shorter events, 122.2 us)
Async XLA Ops:
  7.2 212.6 %copy-start = (bf16[768,768]{1,0:T(8,128)(2,1)S(1)}, bf16[768,768]{1,0:T(8,128)(2,1)}, u32[]{:S(2)}) copy-start(bf16[768,768]{1,0:T(8,128)(2,1)} %param.35) | copy-start | bytes 3538948
  7.2 49.8 %all-gather.9.cloned.1.call-start = ((), (), s32[]{:S(2)}) async-start(), calls=%async_computation | async-start | bytes 6082560 | tf_op jit(solution)/shard_map/all_gather | solution.py:77
  15.9 157.4 %all-gather.13.cloned.1.call-start = ((), (), s32[]{:S(2)}) async-start(), calls=%async_computation.2 | async-start | bytes 6082560 | tf_op jit(solution)/shard_map/all_gather | solution.py:131
  19.1 196.2 %all-gather.11.cloned.1.call-start = ((), (), s32[]{:S(2)}) async-start(), calls=%async_computation.1 | async-start | bytes 6082560 | tf_op jit(solution)/shard_map/all_gather | solution.py:113
  19.4 74.6 %copy-start.6 = (f32[3,197,197]{1,2,0:T(8,128)}, f32[3,197,197]{1,2,0:T(8,128)S(1)}, u32[]{:S(2)}) copy-start(f32[3,197,197]{1,2,0:T(8,128)S(1)} %copy.66) | copy-start | bytes 1397128
  110.1 48.6 %copy-start.40 = (bf16[768]{0:T(1024)(128)(2,1)S(1)}, bf16[768]{0:T(1024)(128)(2,1)}, u32[]{:S(2)}) copy-start(bf16[768]{0:T(1024)(128)(2,1)} %param.32) | copy-start | bytes 4612
  110.1 48.6 %copy-start.41 = (bf16[768]{0:T(1024)(128)(2,1)S(1)}, bf16[768]{0:T(1024)(128)(2,1)}, u32[]{:S(2)}) copy-start(bf16[768]{0:T(1024)(128)(2,1)} %param.31) | copy-start | bytes 4612
  110.1 48.6 %copy-start.42 = (bf16[768]{0:T(1024)(128)(2,1)S(1)}, bf16[768]{0:T(1024)(128)(2,1)}, u32[]{:S(2)}) copy-start(bf16[768]{0:T(1024)(128)(2,1)} %param.33) | copy-start | bytes 4612
  110.1 48.7 %copy-start.43 = (bf16[768]{0:T(1024)(128)(2,1)S(1)}, bf16[768]{0:T(1024)(128)(2,1)}, u32[]{:S(2)}) copy-start(bf16[768]{0:T(1024)(128)(2,1)} %param.34) | copy-start | bytes 4612
  110.1 48.7 %copy-start.46 = (u32[32]{0:T(128)S(1)}, u32[32]{0:T(128)}, u32[]{:S(2)}) copy-start(u32[32]{0:T(128)} %constant.93) | copy-start | bytes 388
  157.4 2.6 collective-permute-start
  173.2 196.8 %all-gather.15.cloned.1.call-start = ((), (), s32[]{:S(2)}) async-start(), calls=%async_computation.3 | async-start | bytes 6082560 | tf_op jit(solution)/shard_map/all_gather | solution.py:157
  215.3 30.8 %slice-start.3 = ((s8[4841472]{0:T(1024)(128)(4,1)}), s8[647168]{0:T(1024)(128)(4,1)S(1)}, s32[]{:S(2)}) async-start(s8[4841472]{0:T(1024)(128)(4,1)} %bitcast.97), calls=%async_computation.8 | async-start | bytes 1294336
  219.8 26.3 %slice-start.4 = ((s8[4841472]{0:T(1024)(128)(4,1)}), s8[4194304]{0:T(1024)(128)(4,1)S(1)}, s32[]{:S(2)}) async-start(s8[4841472]{0:T(1024)(128)(4,1)} %bitcast.97), calls=%async_computation.9 | async-start | bytes 8388608
  219.8 26.3 %copy-start.47 = (bf16[768,768]{1,0:T(8,128)(2,1)S(1)}, bf16[768,768]{1,0:T(8,128)(2,1)}, u32[]{:S(2)}) copy-start(bf16[768,768]{1,0:T(8,128)(2,1)} %param.37) | copy-start | bytes 3538948
  308.6 2.1 collective-permute-start.2
  326.2 10.6 %slice-start.5 = ((s8[4841472]{0:T(1024)(128)(4,1)}), s8[647168]{0:T(1024)(128)(4,1)S(1)}, s32[]{:S(2)}) async-start(s8[4841472]{0:T(1024)(128)(4,1)} %bitcast.99), calls=%async_computation.10 | async-start | bytes 1294336
  327.4 376.3 %all-reduce.14.cloned.1.call-start = ((), (), s32[]{:S(2)}) async-start(), calls=%async_computation.4 | async-start | bytes 15384576 | tf_op jit(solution)/shard_map/psum | solution.py:228
  327.7 9.1 %slice-start.6 = ((s8[4841472]{0:T(1024)(128)(4,1)}), s8[4194304]{0:T(1024)(128)(4,1)S(1)}, s32[]{:S(2)}) async-start(s8[4841472]{0:T(1024)(128)(4,1)} %bitcast.99), calls=%async_computation.11 | async-start | bytes 8388608
  382.3 6.8 copy-start.7
  382.3 6.8 copy-start.25
  389.0 8.2 %copy-start.13 = (bf16[16,197,1,3,64]{1,0,4,3,2:T(8,128)(2,1)S(1)}, bf16[16,197,1,3,64]{1,0,4,3,2:T(8,128)(2,1)}, u32[]{:S(2)}) copy-start(bf16[16,197,1,3,64]{1,0,4,3,2:T(8,128)(2,1)} %copy-done.12) | copy-start | bytes 3631108
  389.1 16.7 %slice-start = ((s8[9830400]{0:T(1024)(128)(4,1)}), s8[4194304]{0:T(1024)(128)(4,1)S(1)}, s32[]{:S(2)}) async-start(s8[9830400]{0:T(1024)(128)(4,1)} %bitcast.95), calls=%async_computation.5 | async-start | bytes 8388608
  389.1 16.7 %slice-start.1 = ((s8[9830400]{0:T(1024)(128)(4,1)}), s8[4194304]{0:T(1024)(128)(4,1)S(1)}, s32[]{:S(2)}) async-start(s8[9830400]{0:T(1024)(128)(4,1)} %bitcast.95), calls=%async_computation.6 | async-start | bytes 8388608
  397.3 8.5 %slice-start.2 = ((s8[9830400]{0:T(1024)(128)(4,1)}), s8[1441792]{0:T(1024)(128)(4,1)S(1)}, s32[]{:S(2)}) async-start(s8[9830400]{0:T(1024)(128)(4,1)} %bitcast.95), calls=%async_computation.7 | async-start | bytes 2883584
  439.8 8.1 %copy-start.27 = (bf16[3152,3,192]{0,2,1:T(8,128)(2,1)}, bf16[3152,3,192]{0,2,1:T(8,128)(2,1)S(1)}, u32[]{:S(2)}) copy-start(bf16[3152,3,192]{0,2,1:T(8,128)(2,1)S(1)} %constant_dynamic-update-slice_fusion) | copy-start | bytes 10893316
  544.2 7.7 %collective-permute-start.3 = (bf16[12,768]{1,0:T(8,128)(2,1)S(1)}, bf16[12,768]{1,0:T(8,128)(2,1)S(1)}, u32[]{:S(2)}, u32[]{:S(2)}) collective-permute-start(bf16[12,768]{1,0:T(8,128)(2,1)S(1)} %slice.20), channel_id=1, source_target_pairs={{0,1},{1,2},{2,3},{4,5},{5,6},{6,7},{8,9},{9,10},{10,11},{12,13},{... | collective-permute-start | bytes 55304
  545.5 13.6 %collective-permute-start.1 = (bf16[12,768]{1,0:T(8,128)(2,1)S(1)}, bf16[12,768]{1,0:T(8,128)(2,1)S(1)}, u32[]{:S(2)}, u32[]{:S(2)}) collective-permute-start(bf16[12,768]{1,0:T(8,128)(2,1)S(1)} %slice.18), channel_id=1, source_target_pairs={{0,1},{1,2},{2,3},{4,5},{5,6},{6,7},{8,9},{9,10},{10,11},{12,13},{... | collective-permute-start | bytes 55304
  551.8 14.4 %copy-start.31 = (f32[788]{0:T(1024)S(1)}, f32[788]{0:T(1024)}, u32[]{:S(2)}) copy-start(f32[788]{0:T(1024)} %copy-done.30) | copy-start | bytes 9460
  551.8 14.4 %copy-start.33 = (f32[768]{0:T(1024)S(1)}, f32[768]{0:T(1024)}, u32[]{:S(2)}) copy-start(f32[768]{0:T(1024)} %copy-done.32) | copy-start | bytes 9220
  551.9 14.4 %copy-start.35 = (f32[788]{0:T(1024)S(1)}, f32[788]{0:T(1024)}, u32[]{:S(2)}) copy-start(f32[788]{0:T(1024)} %copy-done.34) | copy-start | bytes 9460
  559.1 10.3 %copy-start.37 = (f32[768]{0:T(1024)S(1)}, f32[768]{0:T(1024)}, u32[]{:S(2)}) copy-start(f32[768]{0:T(1024)} %copy-done.36) | copy-start | bytes 9220
  (35 other events, 128.5 us)
Sparse Core Ops, SparseCore 0:
  16.0 40.9 all-gather.8
  59.2 38.2 all-gather.12
  173.3 41.9 all-gather.10
  327.6 42.3 all-gather.14
  448.0 255.6 all-reduce.13
where the time goes:
time: 725 us; the launch traced here: 720 us
  blocking collectives  229 us (32%)
  waiting for transfers between devices  165 us (23%)
  matrix products  133 us (18%)
  local copies, waits for them, and re-layouts  122 us (17%)
  other arithmetic  48.1 us (7%)
  between operations  15.5 us (2%)
  starting transfers between devices  7.48 us (1%)
    unnamed x3, blocking collectives  179 us
    psum x1, waiting for transfers between devices, per_device(): lax.psum((row_sums[0], row_sums[1], row_sums[2], qkv_weight_grad, query_b...  74.2 us
    unnamed x136, local copies, waits for them, and re-layouts  68.3 us
    psum x1, blocking collectives, per_device(): lax.psum((row_sums[0], row_sums[1], row_sums[2], qkv_weight_grad, query_b...  39.3 us
    all_gather x1, waiting for transfers between devices, per_device(): first_all = lax.all_gather(first_norm, 'narrow', axis=0, tiled=True)  37.6 us
    all_gather x1, waiting for transfers between devices, per_device(): second_all = lax.all_gather(second_norm, 'narrow', axis=0, tiled=True)  37.2 us
    dot_general x1, matrix products, per_device(): jnp.dot(second_all, up_weight, preferred_element_type=jnp.float32)  26.3 us
    reshape x1, local copies, waits for them, and re-layouts, per_device(): split = triple.reshape(image_count, LEN, 3, head_count, HEAD_DIM)  15.6 us
  transfers between devices with their start and end apart: 9, of which 5 were waited for; matrix products, arithmetic and copies ran while one was open for 38% of the time, Pallas kernels for 0%

commit v1 on v0

v1 whole, which is shorter than its diff:
```python
import functools

import jax
import jax.numpy as jnp
from jax import lax
from jax.experimental import pallas as pl
from jax.experimental.pallas import tpu as pltpu
from jax.sharding import PartitionSpec as P

HEAD_DIM = 64
LEN = 197
PAD = 208
KEYS = 256
EPSILON = 1e-06
HALF_ROOT = 0.7071067811865476
DENSITY_FACTOR = 0.3989422804014327
FAR = -1e30
F32 = jnp.float32
BF16 = jnp.bfloat16
MIB = 1024 * 1024

(MASK_TOKEN, FIRST_GAIN, FIRST_BIAS, OUTPUT_BIAS, ATT_SCALE, SECOND_GAIN, SECOND_BIAS, DOWN_BIAS, FEED_SCALE) = range(9)

NT = (((1,), (1,)), ((), ()))
TN = (((0,), (0,)), ((), ()))
NN = (((1,), (0,)), ((), ()))


def mm(left, right, dims=NN):
    return lax.dot_general(left, right, dims, preferred_element_type=F32)


def call(body, out_shape, flops, bytes_accessed, trans=0, vmem=56, **kw):
    return pl.pallas_call(
        body,
        out_shape=out_shape,
        compiler_params=pltpu.CompilerParams(vmem_limit_bytes=vmem * MIB),
        cost_estimate=pl.CostEstimate(
            flops=int(flops), bytes_accessed=int(bytes_accessed), transcendentals=int(trans)
        ),
        **kw,
    )


def sds(shape, dtype):
    return jax.ShapeDtypeStruct(shape, dtype)


def norm_parts(values):
    average = jnp.mean(values, -1, keepdims=True)
    centered = values - average
    inverse_dev = lax.rsqrt(jnp.mean(centered * centered, -1, keepdims=True) + EPSILON)
    return centered * inverse_dev, inverse_dev


def norm_back(grad_rows, normed, inverse_dev, gain):
    scaled = grad_rows * gain
    return inverse_dev * (
        scaled
        - jnp.mean(scaled, -1, keepdims=True)
        - normed * jnp.mean(scaled * normed, -1, keepdims=True)
    )


def colsum(values):
    return jnp.sum(values, 0, keepdims=True)


def prep_body(images, tok, mask, cot, vec, started_o, first_o, g_o, fg_o, sums_o, wide_s, pad_s):
    width = tok.shape[1]
    rows = tok.shape[0]
    picked = mask[...] == 1.0
    for j in range(width // 128):
        lanes = slice(128 * j, 128 * j + 128)
        wide_s[0:rows, lanes] = jnp.where(
            picked, vec[MASK_TOKEN : MASK_TOKEN + 1, lanes], tok[:, lanes].astype(F32)
        )
    for i in range(images):
        pad_s[0:LEN, :] = wide_s[i * LEN : (i + 1) * LEN, :]
        pad_s[LEN:PAD, :] = jnp.zeros((PAD - LEN, width), F32)
        values = pad_s[...]
        normed, _ = norm_parts(values)
        block = slice(i * PAD, (i + 1) * PAD)
        started_o[block, :] = values.astype(BF16)
        first_o[block, :] = (
            normed * vec[FIRST_GAIN : FIRST_GAIN + 1] + vec[FIRST_BIAS : FIRST_BIAS + 1]
        ).astype(BF16)
    wide_s[0:rows, :] = cot[...].astype(F32)
    total = jnp.zeros((1, width), F32)
    for i in range(images):
        pad_s[0:LEN, :] = wide_s[i * LEN : (i + 1) * LEN, :]
        values = pad_s[...]
        block = slice(i * PAD, (i + 1) * PAD)
        g_o[block, :] = values.astype(BF16)
        feed_grad = (values * vec[FEED_SCALE : FEED_SCALE + 1]).astype(BF16)
        fg_o[block, :] = feed_grad
        total += colsum(feed_grad.astype(F32))
    sums_o[0:1, :] = total
    sums_o[1:8, :] = jnp.zeros((7, width), F32)


def prep(tokens, mask_cols, cotangent, vec):
    rows, width = tokens.shape
    images = rows // LEN
    big = images * PAD
    b = sds((big, width), BF16)
    return call(
        functools.partial(prep_body, images),
        (b, b, b, b, sds((8, width), F32)),
        10 * rows * width,
        6 * 2 * rows * width,
        scratch_shapes=[pltpu.VMEM((-(-rows // 8) * 8, width), F32), pltpu.VMEM((PAD, width), F32)],
    )(tokens, mask_cols, cotangent, vec)


def attention_forward_body(images, local, first, pack_a, pack_b, qkv_o, prob_o, ctx_o, w_s, bias_s):
    pair = 2 * local
    heads = local // HEAD_DIM
    width = first.shape[1]
    big = images * PAD
    score_scale = HEAD_DIM ** (-0.5)
    for t in range(3):
        w_s[t, 0:local, :] = pack_a[t * local : (t + 1) * local, :]
        w_s[t, local:pair, :] = pack_b[t * local : (t + 1) * local, :]
    small = 4 * local + PAD
    shift_q = jnp.concatenate(
        [pack_a[small : small + 16, 0:local], pack_b[small : small + 16, 0:local]], 1
    ).astype(F32)
    for h in range(heads):
        bias_s[h] = pack_a[4 * local : 4 * local + PAD, h * KEYS : (h + 1) * KEYS].astype(F32)
        bias_s[heads + h] = pack_b[4 * local : 4 * local + PAD, h * KEYS : (h + 1) * KEYS].astype(F32)
    for t in range(3):
        value = mm(first[...], w_s[t], NT)
        if t == 0:
            value = value + shift_q[1:2]
        if t == 2:
            value = value + shift_q[2:3]
        qkv_o[t, 0:big, :] = value.astype(BF16)
        qkv_o[t, big:, :] = jnp.zeros((KEYS - PAD, pair), BF16)
    lane = lax.broadcasted_iota(jnp.int32, (1, 128), 1)
    first_half = (lane < HEAD_DIM).astype(BF16)
    halves = (first_half, 1 - first_half)

    def image(i, carry):
        row = pl.multiple_of(i * PAD, 16)
        for tile in range(pair // 128):
            lanes = slice(128 * tile, 128 * tile + 128)
            q = qkv_o[0, pl.ds(row, PAD), lanes]
            k = qkv_o[1, pl.ds(row, KEYS), lanes]
            v = qkv_o[2, pl.ds(row, KEYS), lanes]
            context = None
            for half in range(2):
                head = 2 * tile + half
                scores = mm(q * halves[half], k, NT) * score_scale + bias_s[head]
                top = jnp.max(scores, -1, keepdims=True)
                powers = jnp.exp(scores - top)
                share = 1.0 / jnp.sum(powers, -1, keepdims=True)
                probabilities = (powers * share).astype(BF16)
                prob_o[head, pl.ds(row, PAD), :] = probabilities
                part = mm(probabilities, v * halves[half])
                context = part if context is None else context + part
            ctx_o[pl.ds(row, PAD), lanes] = context.astype(BF16)
        return carry

    lax.fori_loop(0, images, image, 0)


def attention_forward(first, pack_a, pack_b, images, local):
    big, width = first.shape
    pair = 2 * local
    heads = pair // HEAD_DIM
    flops = 2 * big * (width * 3 * pair + 2 * KEYS * HEAD_DIM * heads)
    return call(
        functools.partial(attention_forward_body, images, local),
        (
            sds((3, big + KEYS - PAD, pair), BF16),
            sds((heads, big, KEYS), BF16),
            sds((big, pair), BF16),
        ),
        flops * 2,
        2 * big * (width + 4 * pair + heads * KEYS),
        heads * big * KEYS,
        scratch_shapes=[pltpu.VMEM((3, pair, width), BF16), pltpu.VMEM((heads, PAD, KEYS), F32)],
    )(first, pack_a, pack_b)


def middle_body(images, local, ctx_a, ctx_b, p0, p1, p2, p3, started, vec, branch_o, middle_o, second_o, second_t_o, w_s):
    pair = 2 * local
    for at, pack in enumerate((p0, p1, p2, p3)):
        w_s[at * local : (at + 1) * local, :] = pack[3 * local : 4 * local, :]

    def image(i, carry):
        row = pl.multiple_of(i * PAD, 16)
        block = pl.ds(row, PAD)
        branch = (
            mm(ctx_a[block, :], w_s[0:pair, :])
            + mm(ctx_b[block, :], w_s[pair : 2 * pair, :])
            + vec[OUTPUT_BIAS : OUTPUT_BIAS + 1]
        )
        branch_o[block, :] = branch
        middle = started[block, :].astype(F32) + vec[ATT_SCALE : ATT_SCALE + 1] * branch
        middle_o[block, :] = middle
        normed, _ = norm_parts(middle)
        second_o[block, :] = (
            normed * vec[SECOND_GAIN : SECOND_GAIN + 1] + vec[SECOND_BIAS : SECOND_BIAS + 1]
        ).astype(BF16)
        return carry

    lax.fori_loop(0, images, image, 0)
    second_t_o[...] = second_o[...].T


def middle_stage(ctx_a, ctx_b, packs, started, vec, images, local):
    big, width = started.shape
    return call(
        functools.partial(middle_body, images, local),
        (
            sds((big, width), F32),
            sds((big, width), F32),
            sds((big, width), BF16),
            sds((width, big), BF16),
        ),
        2 * big * width * width + 20 * big * width,
        big * width * 16,
        scratch_shapes=[pltpu.VMEM((4 * local, width), BF16)],
    )(ctx_a, ctx_b, *packs, started, vec)


def feed_body(second, second_t, fg, up, down, up_bias, feed_o, sg_o, dup_o, ddown_o, bias_o, feed_s, sg_s):
    step = pl.program_id(0)
    wu = up[...]
    wd = down[...]
    pre = mm(second[...], wu) + up_bias[0:1, :].astype(F32)
    back = mm(fg[...], wd, NT)
    cdf = 0.5 * (1.0 + lax.erf(pre * HALF_ROOT))
    act = (pre * cdf).astype(BF16)
    slope = cdf + pre * (jnp.exp(-0.5 * pre * pre) * DENSITY_FACTOR)
    pg = (back * slope).astype(BF16)
    feed = mm(act, wd)
    sg = mm(pg, wu, NT)

    @pl.when(step == 0)
    def _():
        feed_s[...] = feed
        sg_s[...] = sg

    @pl.when(step > 0)
    def _():
        feed_s[...] += feed
        sg_s[...] += sg

    ddown_o[...] = mm(act, fg[...], TN).astype(BF16)
    dup_o[...] = mm(second_t[...], pg).astype(BF16)
    bias_o[...] = jnp.broadcast_to(colsum(pg.astype(F32)), bias_o.shape)

    @pl.when(step == pl.num_programs(0) - 1)
    def _():
        feed_o[...] = feed_s[...].astype(BF16)
        sg_o[...] = sg_s[...].astype(BF16)


def feed_stage(second, second_t, fg, up, down, up_bias):
    big, width = second.shape
    hidden = up.shape[1]
    block = 256
    whole = lambda shape: pl.BlockSpec(shape, lambda i: (0, 0))
    return call(
        feed_body,
        (
            sds((big, width), BF16),
            sds((big, width), BF16),
            sds((width, hidden), BF16),
            sds((hidden, width), BF16),
            sds((8, hidden), F32),
        ),
        12 * big * width * hidden,
        2 * (5 * big * width + 4 * hidden * width),
        2 * big * hidden,
        grid=(hidden // block,),
        in_specs=[
            whole((big, width)),
            whole((width, big)),
            whole((big, width)),
            pl.BlockSpec((width, block), lambda i: (0, i)),
            pl.BlockSpec((block, width), lambda i: (i, 0)),
            pl.BlockSpec((16, block), lambda i: (0, i)),
        ],
        out_specs=(
            whole((big, width)),
            whole((big, width)),
            pl.BlockSpec((width, block), lambda i: (0, i)),
            pl.BlockSpec((block, width), lambda i: (i, 0)),
            pl.BlockSpec((8, block), lambda i: (0, i)),
        ),
        scratch_shapes=[pltpu.VMEM((big, width), F32), pltpu.VMEM((big, width), F32)],
    )(second, second_t, fg, up, down, up_bias)


def turn_body(images, parts, *refs):
    feeds = refs[0:parts]
    sgs = refs[parts : 2 * parts]
    middle, branch, g, vec, out_o, mg_o, ag_o, sums_o, wide_s = refs[2 * parts :]
    width = middle.shape[1]
    sums_o[...] = jnp.zeros(sums_o.shape, F32)

    for i in range(images):
        block = slice(i * PAD, (i + 1) * PAD)
        feed = vec[DOWN_BIAS : DOWN_BIAS + 1]
        sg = jnp.zeros((PAD, width), F32)
        for at in range(parts):
            feed = feed + feeds[at][block, :].astype(F32)
            sg = sg + sgs[at][block, :].astype(F32)
        rows = g[block, :].astype(F32)
        mid = middle[block, :]
        out = mid + vec[FEED_SCALE : FEED_SCALE + 1] * feed
        wide_s[i * LEN : (i + 1) * LEN, :] = out[0:LEN]
        normed, inverse = norm_parts(mid)
        grad = rows + norm_back(sg, normed, inverse, vec[SECOND_GAIN : SECOND_GAIN + 1])
        mg_o[block, :] = grad
        att = (vec[ATT_SCALE : ATT_SCALE + 1] * grad).astype(BF16)
        ag_o[block, :] = att
        sums_o[0:1, :] += colsum(rows * feed)
        sums_o[1:2, :] += colsum(sg * normed)
        sums_o[2:3, :] += colsum(sg)
        sums_o[3:4, :] += colsum(grad * branch[block, :])
        sums_o[4:5, :] += colsum(att.astype(F32))
    out_o[...] = wide_s[0 : out_o.shape[0], :].astype(BF16)


def turn_stage(feeds, sgs, middle, branch, g, vec, images):
    big, width = middle.shape
    rows = images * LEN
    return call(
        functools.partial(turn_body, images, len(feeds)),
        (sds((rows, width), BF16), sds((big, width), F32), sds((big, width), BF16), sds((8, width), F32)),
        40 * big * width,
        big * width * (18 + 4 * len(feeds)),
        scratch_shapes=[pltpu.VMEM((-(-rows // 8) * 8, width), F32)],
    )(*feeds, *sgs, middle, branch, g, vec)


def attention_backward_body(
    images, local, first, ag, ctx, qkv, prob, pack_a, pack_b, up_a, up_b,
    grad_a, grad_b, fg_o, w_s, cg_s, tg_s, bias_s, wo_s,
):
    pair = 2 * local
    heads = local // HEAD_DIM
    big, width = first.shape
    score_scale = HEAD_DIM ** (-0.5)
    for t in range(3):
        w_s[t * pair : t * pair + local, :] = pack_a[t * local : (t + 1) * local, :]
        w_s[t * pair + local : (t + 1) * pair, :] = pack_b[t * local : (t + 1) * local, :]
    wo_s[0:local, :] = pack_a[3 * local : 4 * local, :]
    wo_s[local:pair, :] = pack_b[3 * local : 4 * local, :]
    cg_s[0:big, :] = mm(ag[...], wo_s[...], NT).astype(BF16)
    d_out = mm(ctx[...], ag[...], TN).astype(BF16)
    grad_a[3 * local : 4 * local, :] = d_out[0:local]
    grad_b[3 * local : 4 * local, :] = d_out[local:pair]
    bias_s[...] = jnp.zeros(bias_s.shape, F32)
    lane = lax.broadcasted_iota(jnp.int32, (1, 128), 1)
    first_half = (lane < HEAD_DIM).astype(BF16)
    halves = (first_half, 1 - first_half)

    def image(i, carry):
        row = pl.multiple_of(i * PAD, 16)
        for tile in range(pair // 128):
            lanes = slice(128 * tile, 128 * tile + 128)
            q = qkv[0, pl.ds(row, PAD), lanes]
            k = qkv[1, pl.ds(row, KEYS), lanes]
            v = qkv[2, pl.ds(row, KEYS), lanes]
            do = cg_s[pl.ds(row, PAD), lanes]
            dq = dk = dv = None
            for half in range(2):
                head = 2 * tile + half
                p = prob[head, pl.ds(row, PAD), :]
                do_half = do * halves[half]
                dp = mm(do_half, v, NT)
                p32 = p.astype(F32)
                ds = p32 * (dp - jnp.sum(dp * p32, -1, keepdims=True))
                bias_s[head] += ds
                ds = ds.astype(BF16)
                dv_part = mm(p, do_half, TN)
                dk_part = mm(ds, q * halves[half], TN)
                dq_part = mm(ds, k * halves[half])
                dq = dq_part if dq is None else dq + dq_part
                dk = dk_part if dk is None else dk + dk_part
                dv = dv_part if dv is None else dv + dv_part
            block = pl.ds(row, PAD)
            tg_s[block, 128 * tile : 128 * tile + 128] = (dq * score_scale).astype(BF16)
            tg_s[block, pair + 128 * tile : pair + 128 * tile + 128] = (dk[0:PAD] * score_scale).astype(BF16)
            tg_s[block, 2 * pair + 128 * tile : 2 * pair + 128 * tile + 128] = dv[0:PAD].astype(BF16)
        return carry

    lax.fori_loop(0, images, image, 0)
    small = 4 * local + PAD
    grad_a[small:, :] = jnp.zeros((grad_a.shape[0] - small, width), BF16)
    grad_b[small:, :] = jnp.zeros((grad_b.shape[0] - small, width), BF16)
    rows_a = [up_a[0:1, :]]
    rows_b = [up_b[0:1, :]]
    filler = jnp.zeros((1, width - local), F32)
    for t in range(3):
        part = tg_s[:, t * pair : (t + 1) * pair]
        dw = mm(part, first[...], TN).astype(BF16)
        grad_a[t * local : (t + 1) * local, :] = dw[0:local]
        grad_b[t * local : (t + 1) * local, :] = dw[local:pair]
        if t != 1:
            sums = colsum(part.astype(F32))
            rows_a.append(jnp.concatenate([sums[:, 0:local], filler], 1))
            rows_b.append(jnp.concatenate([sums[:, local:pair], filler], 1))
    blank = jnp.zeros((13, width), F32)
    grad_a[small : small + 16, :] = jnp.concatenate(rows_a + [blank], 0).astype(BF16)
    grad_b[small : small + 16, :] = jnp.concatenate(rows_b + [blank], 0).astype(BF16)
    for h in range(heads):
        grad_a[4 * local : 4 * local + PAD, h * KEYS : (h + 1) * KEYS] = bias_s[h].astype(BF16)
        grad_b[4 * local : 4 * local + PAD, h * KEYS : (h + 1) * KEYS] = bias_s[heads + h].astype(BF16)
    fg_o[...] = mm(tg_s[...], w_s[...]).astype(BF16)


def attention_backward(first, ag, ctx, qkv, prob, pack_a, pack_b, up_a, up_b, images, local):
    big, width = first.shape
    pair = 2 * local
    heads = pair // HEAD_DIM
    flops = 2 * big * (8 * width * pair + 8 * KEYS * HEAD_DIM * heads)
    pack = sds(pack_a.shape, BF16)
    return call(
        functools.partial(attention_backward_body, images, local),
        (pack, pack, sds((big, width), BF16)),
        flops * 2,
        2 * big * (3 * width + 5 * pair + heads * KEYS) + 8 * pack_a.size,
        scratch_shapes=[
            pltpu.VMEM((3 * pair, width), BF16),
            pltpu.VMEM((big, pair), BF16),
            pltpu.VMEM((big, 3 * pair), BF16),
            pltpu.VMEM((heads, PAD, KEYS), F32),
            pltpu.VMEM((pair, width), BF16),
        ],
    )(first, ag, ctx, qkv, prob, pack_a, pack_b, up_a, up_b)


def finish_body(images, fg_a, fg_b, mg, started, mask, vec, grad_o, sums_o, wide_s):
    width = mg.shape[1]
    rows = grad_o.shape[0]
    sums_o[...] = jnp.zeros(sums_o.shape, F32)
    for i in range(images):
        block = slice(i * PAD, (i + 1) * PAD)
        fgrad = fg_a[block, :].astype(F32) + fg_b[block, :].astype(F32)
        normed, inverse = norm_parts(started[block, :].astype(F32))
        total = mg[block, :] + norm_back(fgrad, normed, inverse, vec[FIRST_GAIN : FIRST_GAIN + 1])
        sums_o[0:1, :] += colsum(fgrad * normed)
        sums_o[1:2, :] += colsum(fgrad)
        wide_s[i * LEN : (i + 1) * LEN, :] = total[0:LEN]
    picked = mask[...] == 1.0
    for j in range(width // 128):
        lanes = slice(128 * j, 128 * j + 128)
        value = wide_s[0:rows, lanes]
        kept = jnp.where(picked, 0.0, value)
        grad_o[:, lanes] = kept
        sums_o[2:3, lanes] = colsum(value - kept)


def finish_stage(fg_a, fg_b, mg, started, mask_cols, vec, images):
    big, width = mg.shape
    rows = images * LEN
    return call(
        functools.partial(finish_body, images),
        (sds((rows, width), F32), sds((8, width), F32)),
        30 * big * width,
        big * width * 14,
        scratch_shapes=[pltpu.VMEM((-(-rows // 8) * 8, width), F32)],
    )(fg_a, fg_b, mg, started, mask_cols, vec)


def flip(value, axis, size, bit):
    return lax.ppermute(value, axis, [(i, i ^ bit) for i in range(size)])


def added(left, right):
    return (left.astype(F32) + right.astype(F32)).astype(BF16)


def wide_sum(value, wide):
    me = lax.axis_index("wide")
    bits = []
    bit = 1
    while bit < wide:
        bits.append(bit)
        bit *= 2
    for bit in bits:
        half = value.shape[0] // 2
        upper = (me & bit) != 0
        low, high = value[:half], value[half:]
        got = flip(jnp.where(upper, low, high), "wide", wide, bit)
        value = added(jnp.where(upper, high, low), got)
    for bit in bits[::-1]:
        upper = (me & bit) != 0
        got = flip(value, "wide", wide, bit)
        value = jnp.where(
            upper, jnp.concatenate([got, value], 0), jnp.concatenate([value, got], 0)
        )
    return value


def per_device(
    wide,
    narrow,
    tokens,
    patch_mask,
    cotangent,
    mask_token,
    first_gain,
    first_bias,
    qkv_weight,
    query_bias,
    value_bias,
    position_bias,
    output_weight,
    output_bias,
    attention_scale,
    second_gain,
    second_bias,
    up_weight,
    up_bias,
    down_weight,
    down_bias,
    feedforward_scale,
):
    rows, width = tokens.shape
    images = rows // LEN
    local = qkv_weight.shape[2]
    heads = local // HEAD_DIM
    core = functools.partial(flip, axis="narrow", size=narrow, bit=1)
    across = functools.partial(flip, axis="narrow", size=narrow, bit=2)

    qkv_rows = qkv_weight.transpose(1, 2, 0).reshape(3 * local, width)
    bias_rows = jnp.pad(position_bias, ((0, 0), (0, PAD - LEN), (0, KEYS - LEN)), constant_values=FAR)
    bias_rows = bias_rows.transpose(1, 0, 2).reshape(PAD, heads * KEYS)
    small_rows = jnp.concatenate(
        [
            up_bias[None],
            jnp.pad(query_bias[None], ((0, 0), (0, width - local))),
            jnp.pad(value_bias[None], ((0, 0), (0, width - local))),
            jnp.zeros((45, width), BF16),
        ],
        0,
    )
    pack0 = jnp.concatenate([qkv_rows, output_weight, bias_rows, small_rows], 0)
    pack1 = core(pack0)
    pack2 = across(pack0)
    pack3 = core(pack2)
    up1 = core(up_weight)
    down1 = core(down_weight)
    up2 = across(up_weight)
    down2 = across(down_weight)
    up3 = core(up2)
    down3 = core(down2)

    vec = jnp.stack(
        [
            mask_token,
            first_gain,
            first_bias,
            output_bias,
            attention_scale,
            second_gain,
            second_bias,
            down_bias,
            feedforward_scale,
        ]
        + [jnp.zeros_like(mask_token)] * 7
    ).astype(F32)
    mask_cols = jnp.broadcast_to(patch_mask.astype(F32)[:, None], (rows, 128))

    started, first, g, fg, sums_a = prep(tokens, mask_cols, cotangent, vec)
    qkv_a, prob_a, ctx_a = attention_forward(first, pack0, pack1, images, local)
    qkv_b, prob_b, ctx_b = attention_forward(first, pack2, pack3, images, local)
    branch, middle, second, second_t = middle_stage(
        ctx_a, ctx_b, (pack0, pack1, pack2, pack3), started, vec, images, local
    )
    small = 4 * local + PAD
    feeds, sgs, dups, ddowns, dbias = [], [], [], [], []
    for up, down, pack in (
        (up3, down3, pack3),
        (up2, down2, pack2),
        (up1, down1, pack1),
        (up_weight, down_weight, pack0),
    ):
        out = feed_stage(second, second_t, fg, up, down, pack[small : small + 16])
        for to, value in zip((feeds, sgs, dups, ddowns, dbias), out):
            to.append(value)

    layer_out, mg, ag, sums_b = turn_stage(feeds, sgs, middle, branch, g, vec, images)
    grad2, grad3, fg_b = attention_backward(
        first, ag, ctx_b, qkv_b, prob_b, pack2, pack3, dbias[1], dbias[0], images, local
    )
    grad0, grad1, fg_a = attention_backward(
        first, ag, ctx_a, qkv_a, prob_a, pack0, pack1, dbias[3], dbias[2], images, local
    )
    input_grad, sums_c = finish_stage(fg_a, fg_b, mg, started, mask_cols, vec, images)

    def reduced(g3, g2, g1, g0):
        far = added(g2, core(g3))
        got = across(far)
        return wide_sum(added(added(g0, core(g1)), got), wide)

    ddown = reduced(*ddowns)
    dup = reduced(*dups)
    dpack = reduced(grad3, grad2, grad1, grad0)

    vectors = jnp.concatenate([sums_a[0:1], sums_b[0:5], sums_c[0:3], jnp.zeros((7, width), F32)], 0)
    for axis, size in (("narrow", narrow), ("wide", wide)):
        bit = 1
        while bit < size:
            vectors = vectors + flip(vectors, axis, size, bit)
            bit *= 2

    dqkv = dpack[0 : 3 * local].reshape(3, local, width).transpose(2, 0, 1).astype(F32)
    dpos = dpack[4 * local : 4 * local + LEN].reshape(LEN, heads, KEYS)[:, :, :LEN]
    dpos = dpos.transpose(1, 0, 2).astype(F32)
    return (
        layer_out,
        input_grad,
        vectors[8],
        vectors[6],
        vectors[7],
        dqkv,
        dpack[small + 1, 0:local].astype(F32),
        dpack[small + 2, 0:local].astype(F32),
        dpos,
        dpack[3 * local : 4 * local].astype(F32),
        vectors[5],
        vectors[4],
        vectors[2],
        vectors[3],
        dup.astype(F32),
        dpack[small].astype(F32),
        ddown.astype(F32),
        vectors[0],
        vectors[1],
    )


def solution(mesh):
    rows = P(("wide", "narrow"), None)
    in_specs = (
        rows,
        P(("wide", "narrow")),
        rows,
        P(),
        P(),
        P(),
        P(None, None, "narrow"),
        P("narrow"),
        P("narrow"),
        P("narrow", None, None),
        P("narrow", None),
        P(),
        P(),
        P(),
        P(),
        P(None, "narrow"),
        P("narrow"),
        P("narrow", None),
        P(),
        P(),
    )
    out_specs = (
        rows,
        rows,
        P(),
        P(),
        P(),
        P(None, None, "narrow"),
        P("narrow"),
        P("narrow"),
        P("narrow", None, None),
        P("narrow", None),
        P(),
        P(),
        P(),
        P(),
        P(None, "narrow"),
        P("narrow"),
        P("narrow", None),
        P(),
        P(),
    )
    body = functools.partial(per_device, mesh.shape["wide"], mesh.shape["narrow"])
    return jax.shard_map(body, mesh=mesh, in_specs=in_specs, out_specs=out_specs, check_vma=False)
```

time: 725 us -> 461 us (0.64)
  blocking collectives: 229 us -> 0 us
  Pallas kernels: 0 us -> 167 us
  matrix products: 133 us -> 0 us
  local copies, waits for them, and re-layouts: 122 us -> 14.2 us
  starting transfers between devices: 7.48 us -> 49.4 us
  waiting for transfers between devices: 165 us -> 199 us
  other arithmetic: 48.1 us -> 21.8 us
  between operations: 15.5 us -> 1.7 us
    ppermute x0 -> x41, waiting for transfers between devices: none -> 199 us  [flip(): return lax.ppermute(value, axis, [(i, i ^ bit) for i in range(size)])]
    unnamed x3 -> x0, blocking collectives: 179 us -> none
    pallas_call x0 -> x12, Pallas kernels: none -> 167 us  [the longest x4 72.5 us: feed_stage(): call(feed_body, (sds((big, width), BF16), sds((big, width), BF16), sds((w...]
    dot_general x17 -> x0, matrix products: 125 us -> none  [the longest x1 26.3 us: per_device(): jnp.dot(second_all, up_weight, preferred_element_type=jnp.float32)]
    all_gather x4 -> x0, waiting for transfers between devices: 89.9 us -> none  [the longest x1 37.6 us: per_device(): first_all = lax.all_gather(first_norm, 'narrow', axis=0, tiled=True)]
    psum x1 -> x0, waiting for transfers between devices: 74.2 us -> none  [per_device(): lax.psum((row_sums[0], row_sums[1], row_sums[2], qkv_weight_grad, query_b...]
    unnamed x136 -> x49, local copies, waits for them, and re-layouts: 68.3 us -> 3.09 us
    psum x2 -> x0, blocking collectives: 50.2 us -> none  [the longest x1 39.3 us: per_device(): lax.psum((row_sums[0], row_sums[1], row_sums[2], qkv_weight_grad, query_b...]
  transfers between devices with their start and end apart: 9 -> 41, of which waited for: 5 -> 20; matrix products, arithmetic and copies ran while one was open for 38% -> 5% of each run, Pallas kernels for 0% -> 37%
where the time goes in v1:
time: 461 us; the launch traced here: 453 us
  waiting for transfers between devices  199 us (43%)
  Pallas kernels  167 us (36%)
  starting transfers between devices  49.4 us (11%)
  other arithmetic  21.8 us (5%)
  local copies, waits for them, and re-layouts  14.2 us (3%)
    ppermute x41, waiting for transfers between devices, flip(): return lax.ppermute(value, axis, [(i, i ^ bit) for i in range(size)])  199 us
    pallas_call x4, Pallas kernels, feed_stage(): call(feed_body, (sds((big, width), BF16), sds((big, width), BF16), sds((w...  72.5 us
    ppermute x41, starting transfers between devices, flip(): return lax.ppermute(value, axis, [(i, i ^ bit) for i in range(size)])  49.4 us
    pallas_call x2, Pallas kernels, attention_backward(): call(functools.partial(attention_backward_body, images, local), (pack, pa...  38.5 us
    pallas_call x2, Pallas kernels, attention_forward(): call(functools.partial(attention_forward_body, images, local), (sds((3, b...  22.3 us
    pallas_call x1, Pallas kernels, turn_stage(): call(functools.partial(turn_body, images, len(feeds)), (sds((rows, width)...  11.8 us
    convert_element_type x15, other arithmetic, added(): return (left.astype(F32) + right.astype(F32)).astype(BF16)  10.8 us
    pallas_call x1, Pallas kernels, middle_stage(): call(functools.partial(middle_body, images, local), (sds((big, width), F3...  9.4 us
  transfers between devices with their start and end apart: 41, of which 20 were waited for; matrix products, arithmetic and copies ran while one was open for 5% of the time, Pallas kernels for 37%

profile of v1, /device:TPU:0, one launch (start us, length us, event | category | flops | bytes accessed | tf_op | source)
XLA Modules:
  0.0 452.9 jit_solution(8535125630296918063)
XLA Ops:
  5.1 3.0 collective-permute-start.1
  8.2 35.2 %collective-permute-done.1.pack_a.p2 = bf16[1024,768]{1,0:T(8,128)(2,1)} collective-permute-done((bf16[1024,768]{1,0:T(8,128)(2,1)S(1)}, bf16[1024,768]{1,0:T(8,128)(2,1)}, u32[]{:S(2)}, u32[]{:S(2)}) %collective-permute-start.1) | collective-permute-done | bytes 1572896 | tf_op jit(solution)/shard_map/ppermute | solution.py:474
  45.7 23.0 %collective-permute-done.3.up = bf16[768,768]{1,0:T(8,128)(2,1)} collective-permute-done((bf16[768,768]{1,0:T(8,128)(2,1)}, bf16[768,768]{1,0:T(8,128)(2,1)}, u32[]{:S(2)}, u32[]{:S(2)}) %collective-permute-start.3) | collective-permute-done | bytes 1179680 | tf_op jit(solution)/shard_map/ppermute | solution.py:474
  70.6 5.5 %shard_map.339 = (bf16[832,768]{1,0:T(8,128)(2,1)}, bf16[832,768]{1,0:T(8,128)(2,1)}, bf16[832,768]{1,0:T(8,128)(2,1)}, bf16[832,768]{1,0:T(8,128)(2,1)}, f32[8,768]{1,0:T(8,128)}) custom-call(bf16[788,768]{1,0:T(8,128)(2,1)} %tok.1, f32[788,128]{1,0:T(8,128)} %broadcast_in_dim.21.mask, bf16[788,768]{1,0:T(8,128)(2,1)} %cot.1, ...), custom_call_target="tpu_custom_call" | custom-call | flops 6051840 | bytes 7262208 | tf_op jit(solution)/shard_map/pallas_call | solution.py:107
  78.1 15.0 %collective-permute-done.5.down = bf16[768,768]{1,0:T(8,128)(2,1)} collective-permute-done((bf16[768,768]{1,0:T(8,128)(2,1)}, bf16[768,768]{1,0:T(8,128)(2,1)}, u32[]{:S(2)}, u32[]{:S(2)}) %collective-permute-start.5) | collective-permute-done | bytes 1179680 | tf_op jit(solution)/shard_map/ppermute | solution.py:474
  94.3 11.1 %shard_map.340 = (bf16[3,880,384]{2,1,0:T(8,128)(2,1)}, bf16[6,832,256]{2,1,0:T(8,128)(2,1)}, bf16[832,384]{1,0:T(8,128)(2,1)}) custom-call(bf16[832,768]{1,0:T(8,128)(2,1)} %get-tuple-element.66.first, bf16[1024,768]{1,0:T(8,128)(2,1)} %copy-done, bf16[1024,768]{1,0:T(8,128)(2,1)} %copy-done.2), custom_call_target="tpu_custom_call" | custom-call | flops 3598712832 | bytes 6389760 | tf_op jit(solution)/shard_map/pallas_call | solution.py:173
  105.5 11.1 %shard_map.341 = (bf16[3,880,384]{2,1,0:T(8,128)(2,1)}, bf16[6,832,256]{2,1,0:T(8,128)(2,1)}, bf16[832,384]{1,0:T(8,128)(2,1)}) custom-call(bf16[832,768]{1,0:T(8,128)(2,1)} %get-tuple-element.66.first, bf16[1024,768]{1,0:T(8,128)(2,1)} %collective-permute-done.1.pack_a.p2, bf16[1024,768]{1,0:T(8,128)(2,1)} %collective-permute-done.2.pack_b.p3), custom_call_target="tpu_custom_call" | custom-call | flops 3598712832 | bytes 6389760 | tf_op jit(solution)/shard_map/pallas_call | solution.py:173
  116.6 9.4 %shard_map.342 = (f32[832,768]{1,0:T(8,128)}, f32[832,768]{1,0:T(8,128)}, bf16[832,768]{1,0:T(8,128)(2,1)}, bf16[768,832]{1,0:T(8,128)(2,1)}) custom-call(bf16[832,384]{1,0:T(8,128)(2,1)} %get-tuple-element.67.ctx_a.ctx, bf16[832,384]{1,0:T(8,128)(2,1)} %get-tuple-element.68.ctx_b.ctx, bf16[1024,768]{1,0:T(8,128)(2,1)} %copy-done, ...), custom_call_target="tpu_custom_call" | custom-call | flops 994246656 | bytes 10223616 | tf_op jit(solution)/shard_map/pallas_call | solution.py:215
  126.0 15.4 %shard_map.345 = (bf16[832,768]{1,0:T(8,128)(2,1)}, bf16[832,768]{1,0:T(8,128)(2,1)}, bf16[768,768]{1,0:T(8,128)(2,1)}, bf16[768,768]{1,0:T(8,128)(2,1)}, f32[8,768]{1,0:T(8,128)}) custom-call(bf16[832,768]{1,0:T(8,128)(2,1)} %get-tuple-element.70.second, bf16[768,832]{1,0:T(8,128)(2,1)} %get-tuple-element.71.second_t, ...), custom_call_target="tpu_custom_call" | custom-call | flops 5888802816 | bytes 11108352 | tf_op jit(solution)/shard_map/pallas_call | solution.py:267
  143.3 15.1 %shard_map.346 = (bf16[832,768]{1,0:T(8,128)(2,1)}, bf16[832,768]{1,0:T(8,128)(2,1)}, bf16[768,768]{1,0:T(8,128)(2,1)}, bf16[768,768]{1,0:T(8,128)(2,1)}, f32[8,768]{1,0:T(8,128)}) custom-call(bf16[832,768]{1,0:T(8,128)(2,1)} %get-tuple-element.70.second, bf16[768,832]{1,0:T(8,128)(2,1)} %get-tuple-element.71.second_t, ...), custom_call_target="tpu_custom_call" | custom-call | flops 5888802816 | bytes 11108352 | tf_op jit(solution)/shard_map/pallas_call | solution.py:267
  160.5 15.2 %shard_map.343 = (bf16[832,768]{1,0:T(8,128)(2,1)}, bf16[832,768]{1,0:T(8,128)(2,1)}, bf16[768,768]{1,0:T(8,128)(2,1)}, bf16[768,768]{1,0:T(8,128)(2,1)}, f32[8,768]{1,0:T(8,128)}) custom-call(bf16[832,768]{1,0:T(8,128)(2,1)} %get-tuple-element.70.second, bf16[768,832]{1,0:T(8,128)(2,1)} %get-tuple-element.71.second_t, ...), custom_call_target="tpu_custom_call" | custom-call | flops 5888802816 | bytes 11108352 | tf_op jit(solution)/shard_map/pallas_call | solution.py:267
  176.3 26.7 %shard_map.344 = (bf16[832,768]{1,0:T(8,128)(2,1)}, bf16[832,768]{1,0:T(8,128)(2,1)}, bf16[768,768]{1,0:T(8,128)(2,1)}, bf16[768,768]{1,0:T(8,128)(2,1)}, f32[8,768]{1,0:T(8,128)}) custom-call(bf16[832,768]{1,0:T(8,128)(2,1)} %get-tuple-element.70.second, bf16[768,832]{1,0:T(8,128)(2,1)} %get-tuple-element.71.second_t, ...), custom_call_target="tpu_custom_call" | custom-call | flops 5888802816 | bytes 11108352 | tf_op jit(solution)/shard_map/pallas_call | solution.py:267
  203.0 11.8 %shard_map.347 = (bf16[788,768]{1,0:T(8,128)(2,1)}, f32[832,768]{1,0:T(8,128)}, bf16[832,768]{1,0:T(8,128)(2,1)}, f32[8,768]{1,0:T(8,128)}) custom-call(bf16[832,768]{1,0:T(8,128)(2,1)} %get-tuple-element.73.refs_0_, bf16[832,768]{1,0:T(8,128)(2,1)} %get-tuple-element.74.refs_1_, bf16[832,768]{1,0:T(8,128)(2,1)} %get-tuple-element.75.refs_2_, ...), custom_call_target="tpu_custom_call" | custom-call | flops 25559040 | bytes 21725184 | tf_op jit(solution)/shard_map/pallas_call | solution.py:333
  214.9 19.1 %shard_map.349 = (bf16[1024,768]{1,0:T(8,128)(2,1)}, bf16[1024,768]{1,0:T(8,128)(2,1)}, bf16[832,768]{1,0:T(8,128)(2,1)}) custom-call(bf16[832,768]{1,0:T(8,128)(2,1)} %get-tuple-element.66.first, bf16[832,768]{1,0:T(8,128)(2,1)} %get-tuple-element.85.ag, bf16[832,384]{1,0:T(8,128)(2,1)} %get-tuple-element.68.ctx_b.ctx, ...), custom_call_target="tpu_custom_call" | custom-call | flops 10468982784 | bytes 15876096 | tf_op jit(solution)/shard_map/pallas_call | solution.py:425
  237.6 19.4 %shard_map.348 = (bf16[1024,768]{1,0:T(8,128)(2,1)}, bf16[1024,768]{1,0:T(8,128)(2,1)}, bf16[832,768]{1,0:T(8,128)(2,1)}) custom-call(bf16[832,768]{1,0:T(8,128)(2,1)} %get-tuple-element.66.first, bf16[832,768]{1,0:T(8,128)(2,1)} %get-tuple-element.85.ag, bf16[832,384]{1,0:T(8,128)(2,1)} %get-tuple-element.67.ctx_a.ctx, ...), custom_call_target="tpu_custom_call" | custom-call | flops 10468982784 | bytes 15876096 | tf_op jit(solution)/shard_map/pallas_call | solution.py:425
  259.7 3.8 collective-permute-done.25
  268.1 20.6 %collective-permute-done.34 = bf16[768,768]{1,0:T(8,128)(2,1)} collective-permute-done((bf16[768,768]{1,0:T(8,128)(2,1)S(1)}, bf16[768,768]{1,0:T(8,128)(2,1)}, u32[]{:S(2)}, u32[]{:S(2)}) %collective-permute-start.34) | collective-permute-done | bytes 1179680 | tf_op jit(solution)/shard_map/ppermute | solution.py:474
  293.1 6.7 %shard_map.350 = (f32[788,768]{1,0:T(8,128)}, f32[8,768]{1,0:T(8,128)}) custom-call(bf16[832,768]{1,0:T(8,128)(2,1)} %get-tuple-element.90.fg_a, bf16[832,768]{1,0:T(8,128)(2,1)} %get-tuple-element.95.fg_b, f32[832,768]{1,0:T(8,128)} %get-tuple-element.96.mg, bf16[832,768]{1,0:T(8,128)(2,1)} %get-tuple-element.69.started, f32[788,128]{1,0:T(8,128)} %broadcast_in_dim.21.mask, ...), custom_call_target="tpu_custom_call" | custom-call | flops 19169280 | bytes 8945664 | tf_op jit(solution)/shard_map/pallas_call | solution.py:464
  304.9 16.9 %collective-permute-done.16 = bf16[1024,768]{1,0:T(8,128)(2,1)} collective-permute-done((bf16[1024,768]{1,0:T(8,128)(2,1)}, bf16[1024,768]{1,0:T(8,128)(2,1)}, u32[]{:S(2)}, u32[]{:S(2)}) %collective-permute-start.16) | collective-permute-done | bytes 1572896 | tf_op jit(solution)/shard_map/ppermute | solution.py:474
  330.6 6.9 %collective-permute-done.36 = bf16[192,768]{1,0:T(8,128)(2,1)S(1)} collective-permute-done((bf16[192,768]{1,0:T(8,128)(2,1)S(1)}, bf16[192,768]{1,0:T(8,128)(2,1)S(1)}, u32[]{:S(2)}, u32[]{:S(2)}) %collective-permute-start.36) | collective-permute-done | bytes 294944 | tf_op jit(solution)/shard_map/ppermute | solution.py:474
  337.6 5.7 %collective-permute-done.17 = bf16[512,768]{1,0:T(8,128)(2,1)S(1)} collective-permute-done((bf16[512,768]{1,0:T(8,128)(2,1)S(1)}, bf16[512,768]{1,0:T(8,128)(2,1)S(1)}, u32[]{:S(2)}, u32[]{:S(2)}) %collective-permute-start.17) | collective-permute-done | bytes 786464 | tf_op jit(solution)/shard_map/ppermute | solution.py:474
  345.6 2.7 collective-permute-start.37
  348.7 11.0 %collective-permute-done.18 = bf16[256,768]{1,0:T(8,128)(2,1)S(1)} collective-permute-done((bf16[256,768]{1,0:T(8,128)(2,1)S(1)}, bf16[256,768]{1,0:T(8,128)(2,1)S(1)}, u32[]{:S(2)}, u32[]{:S(2)}) %collective-permute-start.18) | collective-permute-done | bytes 393248 | tf_op jit(solution)/shard_map/ppermute | solution.py:474
  363.0 12.0 %collective-permute-done.19 = bf16[128,768]{1,0:T(8,128)(2,1)S(1)} collective-permute-done((bf16[128,768]{1,0:T(8,128)(2,1)S(1)}, bf16[128,768]{1,0:T(8,128)(2,1)S(1)}, u32[]{:S(2)}, u32[]{:S(2)}) %collective-permute-start.19) | collective-permute-done | bytes 196640 | tf_op jit(solution)/shard_map/ppermute | solution.py:474
  377.8 3.6 collective-permute-start.39
  381.4 3.8 collective-permute-done.20
  385.7 2.8 collective-permute-done.30
  390.2 4.6 %collective-permute-done.39 = bf16[192,768]{1,0:T(8,128)(2,1)S(1)} collective-permute-done((bf16[192,768]{1,0:T(8,128)(2,1)S(1)}, bf16[192,768]{1,0:T(8,128)(2,1)S(1)}, u32[]{:S(2)}, u32[]{:S(2)}) %collective-permute-start.39) | collective-permute-done | bytes 294944 | tf_op jit(solution)/shard_map/ppermute | solution.py:474
  396.6 5.6 %collective-permute-done.21 = bf16[256,768]{1,0:T(8,128)(2,1)S(1)} collective-permute-done((bf16[256,768]{1,0:T(8,128)(2,1)S(1)}, bf16[256,768]{1,0:T(8,128)(2,1)S(1)}, u32[]{:S(2)}, u32[]{:S(2)}) %collective-permute-start.21) | collective-permute-done | bytes 393248 | tf_op jit(solution)/shard_map/ppermute | solution.py:474
  408.9 23.7 %collective-permute-done.11 = f32[16,768]{1,0:T(8,128)S(1)} collective-permute-done((f32[16,768]{1,0:T(8,128)S(1)}, f32[16,768]{1,0:T(8,128)S(1)}, u32[]{:S(2)}, u32[]{:S(2)}) %collective-permute-start.11) | collective-permute-done | bytes 49184 | tf_op jit(solution)/shard_map/ppermute | solution.py:474
  434.0 2.7 collective-permute-done.12
  436.7 4.3 collective-permute-start.13
  (194 shorter events, 77.6 us)
Async XLA Ops:
  5.1 38.4 %collective-permute-start.1 = (bf16[1024,768]{1,0:T(8,128)(2,1)S(1)}, bf16[1024,768]{1,0:T(8,128)(2,1)}, u32[]{:S(2)}, u32[]{:S(2)}) collective-permute-start(bf16[1024,768]{1,0:T(8,128)(2,1)S(1)} %concatenate.64.pack_a.p0), channel_id=1, source_target_pairs={{0,2},{1,3},{2,0},{3,1},{4,6},{5,7},{6,4},{7,5},{8,10},{9,11},{10,... | collective-permute-start | bytes 4718600 | tf_op jit(solution)/shard_map/ppermute | solution.py:474
  8.1 60.6 %collective-permute-start.3 = (bf16[768,768]{1,0:T(8,128)(2,1)}, bf16[768,768]{1,0:T(8,128)(2,1)}, u32[]{:S(2)}, u32[]{:S(2)}) collective-permute-start(bf16[768,768]{1,0:T(8,128)(2,1)} %up.1), channel_id=1, source_target_pairs={{0,2},{1,3},{2,0},{3,1},{4,6},{5,7},{6,4},{7,5},{8,10},{9,11},{10,... | collective-permute-start | bytes 3538952 | tf_op jit(solution)/shard_map/ppermute | solution.py:474
  8.2 85.0 %collective-permute-start = (bf16[1024,768]{1,0:T(8,128)(2,1)S(1)}, bf16[1024,768]{1,0:T(8,128)(2,1)S(1)}, u32[]{:S(2)}, u32[]{:S(2)}) collective-permute-start(bf16[1024,768]{1,0:T(8,128)(2,1)S(1)} %concatenate.64.pack_a.p0), channel_id=1, source_target_pairs={{0,1},{1,0},{2,3},{3,2},{4,5},{5,4},{6,7},{7,6},{8,9},{9,8},{10,11... | collective-permute-start | bytes 4718600 | tf_op jit(solution)/shard_map/ppermute | solution.py:474
  43.4 62.0 %collective-permute-start.2 = (bf16[1024,768]{1,0:T(8,128)(2,1)}, bf16[1024,768]{1,0:T(8,128)(2,1)}, u32[]{:S(2)}, u32[]{:S(2)}) collective-permute-start(bf16[1024,768]{1,0:T(8,128)(2,1)} %collective-permute-done.1.pack_a.p2), channel_id=1, source_target_pairs={{0,1},{1,0},{2,3},{3,2},{4,5},{5,4},{6,7},{7,6},{8,9},{9,8},{10,11... | collective-permute-start | bytes 4718600 | tf_op jit(solution)/shard_map/ppermute | solution.py:474
  43.4 49.7 %collective-permute-start.5 = (bf16[768,768]{1,0:T(8,128)(2,1)}, bf16[768,768]{1,0:T(8,128)(2,1)}, u32[]{:S(2)}, u32[]{:S(2)}) collective-permute-start(bf16[768,768]{1,0:T(8,128)(2,1)} %down.1), channel_id=1, source_target_pairs={{0,2},{1,3},{2,0},{3,1},{4,6},{5,7},{6,4},{7,5},{8,10},{9,11},{10,... | collective-permute-start | bytes 3538952 | tf_op jit(solution)/shard_map/ppermute | solution.py:474
  45.5 80.5 %collective-permute-start.7 = (bf16[768,768]{1,0:T(8,128)(2,1)}, bf16[768,768]{1,0:T(8,128)(2,1)}, u32[]{:S(2)}, u32[]{:S(2)}) collective-permute-start(bf16[768,768]{1,0:T(8,128)(2,1)} %up.1), channel_id=1, source_target_pairs={{0,1},{1,0},{2,3},{3,2},{4,5},{5,4},{6,7},{7,6},{8,9},{9,8},{10,11... | collective-permute-start | bytes 3538952 | tf_op jit(solution)/shard_map/ppermute | solution.py:474
  68.7 57.3 %collective-permute-start.8 = (bf16[768,768]{1,0:T(8,128)(2,1)}, bf16[768,768]{1,0:T(8,128)(2,1)}, u32[]{:S(2)}, u32[]{:S(2)}) collective-permute-start(bf16[768,768]{1,0:T(8,128)(2,1)} %down.1), channel_id=1, source_target_pairs={{0,1},{1,0},{2,3},{3,2},{4,5},{5,4},{6,7},{7,6},{8,9},{9,8},{10,11... | collective-permute-start | bytes 3538952 | tf_op jit(solution)/shard_map/ppermute | solution.py:474
  93.2 65.3 %collective-permute-start.4 = (bf16[768,768]{1,0:T(8,128)(2,1)}, bf16[768,768]{1,0:T(8,128)(2,1)S(1)}, u32[]{:S(2)}, u32[]{:S(2)}) collective-permute-start(bf16[768,768]{1,0:T(8,128)(2,1)} %collective-permute-done.3.up), channel_id=1, source_target_pairs={{0,1},{1,0},{2,3},{3,2},{4,5},{5,4},{6,7},{7,6},{8,9},{9,8},{10,11... | collective-permute-start | bytes 3538952 | tf_op jit(solution)/shard_map/ppermute | solution.py:474
  93.2 65.3 %collective-permute-start.6 = (bf16[768,768]{1,0:T(8,128)(2,1)}, bf16[768,768]{1,0:T(8,128)(2,1)S(1)}, u32[]{:S(2)}, u32[]{:S(2)}) collective-permute-start(bf16[768,768]{1,0:T(8,128)(2,1)} %collective-permute-done.5.down), channel_id=1, source_target_pairs={{0,1},{1,0},{2,3},{3,2},{4,5},{5,4},{6,7},{7,6},{8,9},{9,8},{10,11... | collective-permute-start | bytes 3538952 | tf_op jit(solution)/shard_map/ppermute | solution.py:474
  141.4 117.2 %collective-permute-start.23 = (bf16[768,768]{1,0:T(8,128)(2,1)}, bf16[768,768]{1,0:T(8,128)(2,1)}, u32[]{:S(2)}, u32[]{:S(2)}) collective-permute-start(bf16[768,768]{1,0:T(8,128)(2,1)} %get-tuple-element.106), channel_id=1, source_target_pairs={{0,1},{1,0},{2,3},{3,2},{4,5},{5,4},{6,7},{7,6},{8,9},{9,8},{10,11... | collective-permute-start | bytes 3538952 | tf_op jit(solution)/shard_map/ppermute | solution.py:474
  141.9 126.2 %collective-permute-start.32 = (bf16[768,768]{1,0:T(8,128)(2,1)}, bf16[768,768]{1,0:T(8,128)(2,1)S(1)}, u32[]{:S(2)}, u32[]{:S(2)}) collective-permute-start(bf16[768,768]{1,0:T(8,128)(2,1)} %get-tuple-element.110), channel_id=1, source_target_pairs={{0,1},{1,0},{2,3},{3,2},{4,5},{5,4},{6,7},{7,6},{8,9},{9,8},{10,11... | collective-permute-start | bytes 3538952 | tf_op jit(solution)/shard_map/ppermute | solution.py:474
  175.8 58.4 %collective-permute-start.24 = (bf16[768,768]{1,0:T(8,128)(2,1)}, bf16[768,768]{1,0:T(8,128)(2,1)S(1)}, u32[]{:S(2)}, u32[]{:S(2)}) collective-permute-start(bf16[768,768]{1,0:T(8,128)(2,1)} %get-tuple-element.108), channel_id=1, source_target_pairs={{0,1},{1,0},{2,3},{3,2},{4,5},{5,4},{6,7},{7,6},{8,9},{9,8},{10,11... | collective-permute-start | bytes 3538952 | tf_op jit(solution)/shard_map/ppermute | solution.py:474
  176.3 60.0 %collective-permute-start.33 = (bf16[768,768]{1,0:T(8,128)(2,1)}, bf16[768,768]{1,0:T(8,128)(2,1)S(1)}, u32[]{:S(2)}, u32[]{:S(2)}) collective-permute-start(bf16[768,768]{1,0:T(8,128)(2,1)} %get-tuple-element.112), channel_id=1, source_target_pairs={{0,1},{1,0},{2,3},{3,2},{4,5},{5,4},{6,7},{7,6},{8,9},{9,8},{10,11... | collective-permute-start | bytes 3538952 | tf_op jit(solution)/shard_map/ppermute | solution.py:474
  233.9 23.1 %collective-permute-start.15 = (bf16[1024,768]{1,0:T(8,128)(2,1)}, bf16[1024,768]{1,0:T(8,128)(2,1)S(1)}, u32[]{:S(2)}, u32[]{:S(2)}) collective-permute-start(bf16[1024,768]{1,0:T(8,128)(2,1)} %get-tuple-element.104), channel_id=1, source_target_pairs={{0,1},{1,0},{2,3},{3,2},{4,5},{5,4},{6,7},{7,6},{8,9},{9,8},{10,11... | collective-permute-start | bytes 4718600 | tf_op jit(solution)/shard_map/ppermute | solution.py:474
  234.5 29.0 %collective-permute-start.25 = (bf16[768,768]{1,0:T(8,128)(2,1)S(1)}, bf16[768,768]{1,0:T(8,128)(2,1)}, u32[]{:S(2)}, u32[]{:S(2)}) collective-permute-start(bf16[768,768]{1,0:T(8,128)(2,1)S(1)} %add_convert_fusion.7), channel_id=1, source_target_pairs={{0,2},{1,3},{2,0},{3,1},{4,6},{5,7},{6,4},{7,5},{8,10},{9,11},{10,... | collective-permute-start | bytes 3538952 | tf_op jit(solution)/shard_map/ppermute | solution.py:474
  236.6 52.1 %collective-permute-start.34 = (bf16[768,768]{1,0:T(8,128)(2,1)S(1)}, bf16[768,768]{1,0:T(8,128)(2,1)}, u32[]{:S(2)}, u32[]{:S(2)}) collective-permute-start(bf16[768,768]{1,0:T(8,128)(2,1)S(1)} %add_convert_fusion.4), channel_id=1, source_target_pairs={{0,2},{1,3},{2,0},{3,1},{4,6},{5,7},{6,4},{7,5},{8,10},{9,11},{10,... | collective-permute-start | bytes 3538952 | tf_op jit(solution)/shard_map/ppermute | solution.py:474
  257.0 47.9 %collective-permute-start.14 = (bf16[1024,768]{1,0:T(8,128)(2,1)}, bf16[1024,768]{1,0:T(8,128)(2,1)}, u32[]{:S(2)}, u32[]{:S(2)}) collective-permute-start(bf16[1024,768]{1,0:T(8,128)(2,1)} %get-tuple-element.102), channel_id=1, source_target_pairs={{0,1},{1,0},{2,3},{3,2},{4,5},{5,4},{6,7},{7,6},{8,9},{9,8},{10,11... | collective-permute-start | bytes 4718600 | tf_op jit(solution)/shard_map/ppermute | solution.py:474
  258.6 63.2 %collective-permute-start.16 = (bf16[1024,768]{1,0:T(8,128)(2,1)}, bf16[1024,768]{1,0:T(8,128)(2,1)}, u32[]{:S(2)}, u32[]{:S(2)}) collective-permute-start(bf16[1024,768]{1,0:T(8,128)(2,1)} %add_convert_fusion.1), channel_id=1, source_target_pairs={{0,2},{1,3},{2,0},{3,1},{4,6},{5,7},{6,4},{7,5},{8,10},{9,11},{10,... | collective-permute-start | bytes 4718600 | tf_op jit(solution)/shard_map/ppermute | solution.py:474
  266.4 34.2 %collective-permute-start.26 = (bf16[384,768]{1,0:T(8,128)(2,1)}, bf16[384,768]{1,0:T(8,128)(2,1)}, u32[]{:S(2)}, u32[]{:S(2)}) collective-permute-start(bf16[384,768]{1,0:T(8,128)(2,1)} %broadcast_select_fusion.2), channel_id=1, source_target_pairs={{0,4},{4,0},{8,12},{12,8},{16,20},{20,16},{24,28},{28,24},{1,5},{5... | collective-permute-start | bytes 1769480 | tf_op jit(solution)/shard_map/ppermute | solution.py:474
  302.0 25.9 %collective-permute-start.27 = (bf16[192,768]{1,0:T(8,128)(2,1)S(1)}, bf16[192,768]{1,0:T(8,128)(2,1)S(1)}, u32[]{:S(2)}, u32[]{:S(2)}) collective-permute-start(bf16[192,768]{1,0:T(8,128)(2,1)S(1)} %broadcast_select_fusion.5), channel_id=1, source_target_pairs={{0,8},{4,12},{8,0},{12,4},{16,24},{20,28},{24,16},{28,20},{1,9},{5... | collective-permute-start | bytes 884744 | tf_op jit(solution)/shard_map/ppermute | solution.py:474
  324.4 19.0 %collective-permute-start.17 = (bf16[512,768]{1,0:T(8,128)(2,1)S(1)}, bf16[512,768]{1,0:T(8,128)(2,1)S(1)}, u32[]{:S(2)}, u32[]{:S(2)}) collective-permute-start(bf16[512,768]{1,0:T(8,128)(2,1)S(1)} %broadcast_select_fusion), channel_id=1, source_target_pairs={{0,4},{4,0},{8,12},{12,8},{16,20},{20,16},{24,28},{28,24},{1,5},{5... | collective-permute-start | bytes 2359304 | tf_op jit(solution)/shard_map/ppermute | solution.py:474
  328.0 20.3 %collective-permute-start.28 = (bf16[96,768]{1,0:T(8,128)(2,1)S(1)}, bf16[96,768]{1,0:T(8,128)(2,1)S(1)}, u32[]{:S(2)}, u32[]{:S(2)}) collective-permute-start(bf16[96,768]{1,0:T(8,128)(2,1)S(1)} %broadcast_select_fusion.8), channel_id=1, source_target_pairs={{0,16},{4,20},{8,24},{12,28},{16,0},{20,4},{24,8},{28,12},{1,17},{... | collective-permute-start | bytes 442376 | tf_op jit(solution)/shard_map/ppermute | solution.py:474
  343.7 16.0 %collective-permute-start.18 = (bf16[256,768]{1,0:T(8,128)(2,1)S(1)}, bf16[256,768]{1,0:T(8,128)(2,1)S(1)}, u32[]{:S(2)}, u32[]{:S(2)}) collective-permute-start(bf16[256,768]{1,0:T(8,128)(2,1)S(1)} %broadcast_select_fusion.3), channel_id=1, source_target_pairs={{0,8},{4,12},{8,0},{12,4},{16,24},{20,28},{24,16},{28,20},{1,9},{5... | collective-permute-start | bytes 1179656 | tf_op jit(solution)/shard_map/ppermute | solution.py:474
  345.6 16.3 %collective-permute-start.37 = (bf16[96,768]{1,0:T(8,128)(2,1)S(1)}, bf16[96,768]{1,0:T(8,128)(2,1)S(1)}, u32[]{:S(2)}, u32[]{:S(2)}) collective-permute-start(bf16[96,768]{1,0:T(8,128)(2,1)S(1)} %broadcast_select_fusion.7), channel_id=1, source_target_pairs={{0,16},{4,20},{8,24},{12,28},{16,0},{20,4},{24,8},{28,12},{1,17},{... | collective-permute-start | bytes 442376 | tf_op jit(solution)/shard_map/ppermute | solution.py:474
  348.3 26.9 %collective-permute-start.29 = (bf16[96,768]{1,0:T(8,128)(2,1)S(1)}, bf16[96,768]{1,0:T(8,128)(2,1)S(1)}, u32[]{:S(2)}, u32[]{:S(2)}) collective-permute-start(bf16[96,768]{1,0:T(8,128)(2,1)S(1)} %add_convert_fusion.17), channel_id=1, source_target_pairs={{0,16},{4,20},{8,24},{12,28},{16,0},{20,4},{24,8},{28,12},{1,17},{... | collective-permute-start | bytes 442376 | tf_op jit(solution)/shard_map/ppermute | solution.py:474
  377.8 17.1 %collective-permute-start.39 = (bf16[192,768]{1,0:T(8,128)(2,1)S(1)}, bf16[192,768]{1,0:T(8,128)(2,1)S(1)}, u32[]{:S(2)}, u32[]{:S(2)}) collective-permute-start(bf16[192,768]{1,0:T(8,128)(2,1)S(1)} %maximum_select_fusion.8), channel_id=1, source_target_pairs={{0,8},{4,12},{8,0},{12,4},{16,24},{20,28},{24,16},{28,20},{1,9},{5... | collective-permute-start | bytes 884744 | tf_op jit(solution)/shard_map/ppermute | solution.py:474
  385.2 17.0 %collective-permute-start.21 = (bf16[256,768]{1,0:T(8,128)(2,1)S(1)}, bf16[256,768]{1,0:T(8,128)(2,1)S(1)}, u32[]{:S(2)}, u32[]{:S(2)}) collective-permute-start(bf16[256,768]{1,0:T(8,128)(2,1)S(1)} %maximum_select_fusion.6), channel_id=1, source_target_pairs={{0,8},{4,12},{8,0},{12,4},{16,24},{20,28},{24,16},{28,20},{1,9},{5... | collective-permute-start | bytes 1179656 | tf_op jit(solution)/shard_map/ppermute | solution.py:474
  385.7 18.4 %collective-permute-start.9 = (f32[16,768]{1,0:T(8,128)S(1)}, f32[16,768]{1,0:T(8,128)S(1)}, u32[]{:S(2)}, u32[]{:S(2)}) collective-permute-start(f32[16,768]{1,0:T(8,128)S(1)} %maximum_maximum_fusion), channel_id=1, source_target_pairs={{0,1},{1,0},{2,3},{3,2},{4,5},{5,4},{6,7},{7,6},{8,9},{9,8},{10,11... | collective-permute-start | bytes 147464 | tf_op jit(solution)/shard_map/ppermute | solution.py:474
  388.7 55.1 %collective-permute-start.31 = (bf16[384,768]{1,0:T(8,128)(2,1)S(1)}, bf16[384,768]{1,0:T(8,128)(2,1)S(1)}, u32[]{:S(2)}, u32[]{:S(2)}) collective-permute-start(bf16[384,768]{1,0:T(8,128)(2,1)S(1)} %maximum_select_fusion.4), channel_id=1, source_target_pairs={{0,4},{4,0},{8,12},{12,8},{16,20},{20,16},{24,28},{28,24},{1,5},{5... | collective-permute-start | bytes 1769480 | tf_op jit(solution)/shard_map/ppermute | solution.py:474
  395.0 50.4 %collective-permute-start.40 = (bf16[384,768]{1,0:T(8,128)(2,1)S(1)}, bf16[384,768]{1,0:T(8,128)(2,1)S(1)}, u32[]{:S(2)}, u32[]{:S(2)}) collective-permute-start(bf16[384,768]{1,0:T(8,128)(2,1)S(1)} %maximum_select_fusion.5), channel_id=1, source_target_pairs={{0,4},{4,0},{8,12},{12,8},{16,20},{20,16},{24,28},{28,24},{1,5},{5... | collective-permute-start | bytes 1769480 | tf_op jit(solution)/shard_map/ppermute | solution.py:474
  402.5 44.5 %collective-permute-start.22 = (bf16[512,768]{1,0:T(8,128)(2,1)S(1)}, bf16[512,768]{1,0:T(8,128)(2,1)S(1)}, u32[]{:S(2)}, u32[]{:S(2)}) collective-permute-start(bf16[512,768]{1,0:T(8,128)(2,1)S(1)} %maximum_select_fusion.3), channel_id=1, source_target_pairs={{0,4},{4,0},{8,12},{12,8},{16,20},{20,16},{24,28},{28,24},{1,5},{5... | collective-permute-start | bytes 2359304 | tf_op jit(solution)/shard_map/ppermute | solution.py:474
  408.3 24.3 %collective-permute-start.11 = (f32[16,768]{1,0:T(8,128)S(1)}, f32[16,768]{1,0:T(8,128)S(1)}, u32[]{:S(2)}, u32[]{:S(2)}) collective-permute-start(f32[16,768]{1,0:T(8,128)S(1)} %add.76), channel_id=1, source_target_pairs={{0,4},{4,0},{8,12},{12,8},{16,20},{20,16},{24,28},{28,24},{1,5},{5... | collective-permute-start | bytes 147464 | tf_op jit(solution)/shard_map/ppermute | solution.py:474
  (34 other events, 940.7 us)
